TPU v7x, 512 devices: a whole 4x8x8 slice. The times are simulated.
512 devices in a mesh: tile: 64 (over y, x, core), chan: 8 (over z).
Axes of the slice: x: 4, y: 8, z: 8, core: 2. Of those that a mesh axis runs over, the one named last changes fastest.
Arguments:
- activations: bfloat16 [64, 128, 4096], P('tile', 'chan'), may hold values from -6 to 6
- cotangent: bfloat16 [64, 128, 4096], P('tile', 'chan'), may hold values from -6 to 6
- kernel: float32 [128, 49], P('chan'), may hold values from -0.875 to 0.875
- gain: float32 [128], replicated, may hold values from 0.25 to 2
- w_in: bfloat16 [128, 512], P(None, 'chan'), may hold values from -0.5 to 0.5
- w_out: bfloat16 [512, 128], P('chan'), may hold values from -0.25 to 0.25
- neighbours: int32 [64, 8], P('tile'), may hold values from -1 to 63, as said below
- land_mask: int32 [64, 4096], P('tile'), may hold values 0 or 1
Outputs:
- output: bfloat16 [64, 128, 4096], P('tile', 'chan')
- input_grad: bfloat16 [64, 128, 4096], P('tile', 'chan')
- kernel_grad: float32 [128, 49], P('chan')
- gain_grad: float32 [128], P('chan')
- w_in_grad: float32 [128, 512], P(None, 'chan')
- w_out_grad: float32 [512, 128], P('chan')
Inputs may be any that keep to these rules, and one draw needn't show every extreme that they name: neighbours[s, k] is the ocean tile beside tile s in direction k, tiles lying on a grid whose columns wrap around and whose top and bottom rows have nothing beyond; -1 for land or beyond the grid; if t is beside s in one direction then s is beside t in the opposite one.
All inputs are finite; a program needn't handle non-finite values. No bound on the sum of `land_mask` on one device may be relied on, other than what follows from the above.
Results may differ from a plain program's by a relative error of at most 0.019.
Values may be sent and summed in bfloat16 or wider, within the bound.
A program may use at most 64 MiB of HBM per device.

v0:
```python
import jax
import jax.numpy as jnp
from jax import lax
from jax.sharding import PartitionSpec as P

C = 128
SIDE = 64


EPS = 1e-06


def rim_strips(grid):
    count, chans, side, _ = grid.shape
    top = grid[:, :, :3, :]
    bottom = grid[:, :, side - 3 :, :]
    left = jnp.swapaxes(grid[:, :, :, :3], 2, 3)
    right = jnp.swapaxes(grid[:, :, :, side - 3 :], 2, 3)
    return jnp.stack([top, bottom, left, right], 2).reshape(count, chans, 12 * side)


def assemble(center, near):
    side = center.shape[-1]
    above = near[:, 0:3, :, 1]
    below = near[:, 5:8, :, 0]
    west = jnp.swapaxes(near[:, 3, :, 3], 2, 3)
    east = jnp.swapaxes(near[:, 4, :, 2], 2, 3)
    top_row = jnp.concatenate(
        [above[:, 0, :, :, side - 3 :], above[:, 1], above[:, 2, :, :, :3]], -1
    )
    middle = jnp.concatenate([west, center, east], -1)
    bottom_row = jnp.concatenate(
        [below[:, 0, :, :, side - 3 :], below[:, 1], below[:, 2, :, :, :3]], -1
    )
    return jnp.concatenate([top_row, middle, bottom_row], 2)


def depthwise(padded, kernel):
    side = padded.shape[-1] - 6
    total = jnp.zeros(padded.shape[:2] + (side, side), jnp.float32)
    for row in range(7):
        for col in range(7):
            total = total + kernel[None, :, row * 7 + col, None, None] * padded[
                :, :, row : row + side, col : col + side
            ].astype(jnp.float32)
    return total


def flipped(padded, kernel):
    side = padded.shape[-1] - 6
    total = jnp.zeros(padded.shape[:2] + (side, side), jnp.float32)
    for row in range(7):
        for col in range(7):
            total = total + kernel[None, :, row * 7 + col, None, None] * padded[
                :, :, 6 - row : 6 - row + side, 6 - col : 6 - col + side
            ].astype(jnp.float32)
    return total


def kernel_grad_of(padded, grads):
    side = grads.shape[-1]
    weights = grads.astype(jnp.float32)
    columns = []
    for row in range(7):
        for col in range(7):
            columns.append(
                jnp.sum(
                    weights * padded[:, :, row : row + side, col : col + side].astype(jnp.float32),
                    axis=(0, 2, 3),
                )
            )
    return jnp.stack(columns, 1)


def gelu_pair(pre):
    inner = 0.7978845608 * (pre + 0.044715 * pre * pre * pre)
    bend = jnp.tanh(inner)
    value = 0.5 * pre * (1.0 + bend)
    slope = 0.5 * (1.0 + bend) + 0.5 * pre * (1.0 - bend * bend) * 0.7978845608 * (
        1.0 + 3.0 * 0.044715 * pre * pre
    )
    return (value, slope)


def pick_rims(table, slots, local, chans, side):
    extended = jnp.concatenate([table, jnp.zeros((1, chans, 12 * side), table.dtype)], 0)
    return extended[slots].reshape(local, 8, chans, 4, 3, side)


def body(activations, cotangent, kernel, gain, w_in, w_out, neighbours, land_mask):
    local, mine_chans, cells = activations.shape
    side = SIDE
    chans = C
    member = lax.axis_index("chan")
    total_tiles = local * lax.axis_size("tile")
    slots = jnp.where(neighbours < 0, total_tiles, neighbours)
    grid = activations.reshape(local, mine_chans, side, side)
    table = lax.all_gather(rim_strips(grid), "tile", axis=0, tiled=True)
    padded = assemble(grid, pick_rims(table, slots, local, mine_chans, side))
    conv = depthwise(padded, kernel).reshape(local, mine_chans, cells)
    mask = land_mask.astype(jnp.float32)
    gain_mine = lax.dynamic_slice_in_dim(gain, member * mine_chans, mine_chans)
    total_value, total_square = lax.psum((jnp.sum(conv, 1), jnp.sum(conv * conv, 1)), "chan")
    mean = total_value / chans
    rstd = lax.rsqrt(total_square / chans - mean * mean + EPS)
    normed = (conv - mean[:, None, :]) * rstd[:, None, :]
    feats_mine = (normed * gain_mine[None, :, None]).astype(jnp.bfloat16)
    feats = lax.all_gather(feats_mine, "chan", axis=1, tiled=True)
    pre = jnp.einsum("ch,tcp->thp", w_in, feats, preferred_element_type=jnp.float32)
    value, slope = gelu_pair(pre)
    act = value.astype(jnp.bfloat16)
    terms = jnp.einsum("hc,thp->tcp", w_out, act, preferred_element_type=jnp.float32)
    residual_branch = lax.psum_scatter(
        terms.astype(jnp.bfloat16), "chan", scatter_dimension=1, tiled=True
    ).astype(jnp.float32)
    output = (activations.astype(jnp.float32) + mask[:, None, :] * residual_branch).astype(
        jnp.bfloat16
    )
    masked_mine = (cotangent.astype(jnp.float32) * mask[:, None, :]).astype(jnp.bfloat16)
    masked = lax.all_gather(masked_mine, "chan", axis=1, tiled=True)
    grad_out = jnp.einsum("thp,tcp->hc", act, masked, preferred_element_type=jnp.float32)
    d_act = jnp.einsum("hc,tcp->thp", w_out, masked, preferred_element_type=jnp.float32)
    d_pre = (d_act * slope).astype(jnp.bfloat16)
    grad_in = jnp.einsum("tcp,thp->ch", feats, d_pre, preferred_element_type=jnp.float32)
    feat_terms = jnp.einsum("ch,thp->tcp", w_in, d_pre, preferred_element_type=jnp.float32)
    feature_cotangent = lax.psum_scatter(
        feat_terms.astype(jnp.bfloat16), "chan", scatter_dimension=1, tiled=True
    ).astype(jnp.float32)
    grad_gain = jnp.sum(feature_cotangent * normed, axis=(0, 2))
    d_norm = feature_cotangent * gain_mine[None, :, None]
    first, second = lax.psum((jnp.sum(d_norm, 1), jnp.sum(d_norm * normed, 1)), "chan")
    d_conv = (
        rstd[:, None, :]
        * (d_norm - first[:, None, :] / chans - normed * second[:, None, :] / chans)
    ).astype(jnp.bfloat16)
    dgrid = d_conv.reshape(local, mine_chans, side, side)
    grad_kernel = kernel_grad_of(padded, dgrid)
    dtable = lax.all_gather(rim_strips(dgrid), "tile", axis=0, tiled=True)
    dpadded = assemble(dgrid, pick_rims(dtable, slots, local, mine_chans, side))
    back = flipped(dpadded, kernel).reshape(local, mine_chans, cells)
    input_grad = (cotangent.astype(jnp.float32) + back).astype(jnp.bfloat16)
    grad_in, grad_out, grad_gain, grad_kernel = lax.psum(
        (grad_in, grad_out, grad_gain, grad_kernel), "tile"
    )
    return (output, input_grad, grad_kernel, grad_gain, grad_in, grad_out)


def solution(mesh):
    placed = (
        P("tile", "chan", None),
        P("tile", "chan", None),
        P("chan", None),
        P(),
        P(None, "chan"),
        P("chan", None),
        P("tile", None),
        P("tile", None),
    )
    return jax.shard_map(
        body,
        mesh=mesh,
        in_specs=placed,
        out_specs=(
            P("tile", "chan", None),
            P("tile", "chan", None),
            P("chan", None),
            P("chan"),
            P(None, "chan"),
            P("chan", None),
        ),
        check_vma=False,
    )
```

profile of v0, /device:TPU:1, one launch (start us, length us, event | category | flops | bytes accessed | tf_op | source)
XLA Modules:
  0.0 665.5 jit_solution(2718711398868422744)
XLA Ops:
  13.1 86.9 %all-gather.5.cloned.1.call-done = bf16[64,16,768]{2,1,0:T(8,128)(2,1)} async-done(((bf16[1,16,768]{2,1,0:T(8,128)(2,1)}), bf16[64,16,768]{2,1,0:T(8,128)(2,1)}) %all-gather.5.cloned.1.call-update) | async-done | bytes 1572880 | tf_op jit(solution)/shard_map/all_gather | solution.py:98
  100.0 1.5 concatenate.138
  104.1 6.9 %fusion.152 = (f32[64,64]{1,0:T(8,128)S(1)}, f32[64,64]{1,0:T(8,128)S(1)}, f32[1,16,64,64]{3,2,1,0:T(8,128)S(1)}) fusion(bf16[1,16,67,70]{3,2,1,0:T(8,128)(2,1)S(1)} %get-tuple-element.149, f32[16]{0:T(128)S(1)} %get-tuple-element.130, f32[16]{0:T(128)S(1)} %get-tuple-element.131, f32[16]{0:T(128)S(1)} %get-tuple-element.84, f32[16]{0:T(128)S(1)} %get-tuple-element.85, ...), kind=kLoop, calls=%fused_computation.358 | loop fusion | flops 10936320 | bytes 5946432 | tf_op jit(solution)/shard_map/reduce_sum | solution.py:103
  111.3 23.7 %all-reduce.6 = (f32[1,4096]{1,0:T(1,128)S(1)}, f32[1,4096]{1,0:T(1,128)S(1)}) all-reduce(f32[1,4096]{1,0:T(1,128)S(1)} %reduce_sum.497, f32[1,4096]{1,0:T(1,128)S(1)} %reduce_sum.495), channel_id=1, replica_groups=mesh['tile'=64,'chan'=8] {'chan'}, use_global_device_ids=true, to_apply=%region_3.4 | all-reduce | flops 8192 | bytes 65536 | tf_op jit(solution)/shard_map/psum | solution.py:103
  136.7 38.5 %all-gather.7.cloned.1.call-done = bf16[1,128,4096]{2,1,0:T(8,128)(2,1)} async-done(((bf16[1,16,4096]{2,1,0:T(8,128)(2,1)}), bf16[1,128,4096]{2,1,0:T(8,128)(2,1)}) %all-gather.7.cloned.1.call-update) | async-done | bytes 1048592 | tf_op jit(solution)/shard_map/all_gather | solution.py:108
  175.2 1.5 convolution_bitcast_fusion.1
  176.7 1.6 fusion
  178.3 39.9 %all-gather.9.cloned.1.call-done = bf16[1,128,4096]{2,1,0:T(8,128)(2,1)} async-done(((bf16[1,16,4096]{2,1,0:T(8,128)(2,1)}), bf16[1,128,4096]{2,1,0:T(8,128)(2,1)}) %all-gather.9.cloned.1.call-update) | async-done | bytes 1048592 | tf_op jit(solution)/shard_map/all_gather | solution.py:120
  218.2 2.1 fusion.4
  220.7 4.2 copy.350
  225.0 5.5 copy.348
  232.5 116.5 %all-reduce.13.cloned.1.call-done = (bf16[1,128,4096]{2,0,1:T(2,128)(2,1)}, bf16[1,128,4096]{2,0,1:T(2,128)(2,1)}) async-done(((bf16[1,128,4096]{2,0,1:T(2,128)(2,1)}, bf16[1,128,4096]{2,0,1:T(2,128)(2,1)}), (bf16[1,128,4096]{2,0,1:T(2,128)(2,1)}, bf16[1,128,4096]{2,0,1:T(2,128)(2,1)})) %all-reduce.13.cloned.1.call-update) | async-done | bytes 2097168
  352.3 21.3 %all-reduce.5 = (f32[4096]{0:T(1024)S(1)}, f32[1,4096]{1,0:T(1,128)S(1)}) all-reduce(f32[4096]{0:T(1024)S(1)} %get-tuple-element.72, f32[1,4096]{1,0:T(1,128)S(1)} %bitcast.201), channel_id=1, replica_groups=mesh['tile'=64,'chan'=8] {'chan'}, use_global_device_ids=true, to_apply=%region_9.10 | all-reduce | flops 8192 | bytes 65536 | tf_op jit(solution)/shard_map/psum | solution.py:131
  373.6 1.5 fusion.143
  377.4 2.4 pad_maximum_fusion.1
  379.8 1.7 copy.354
  383.6 2.7 fusion.10
  386.3 2.3 fusion.135
  388.8 2.9 fusion.109
  391.9 2.9 fusion.136
  399.3 72.0 %all-gather.11.cloned.1.call-done = bf16[64,16,768]{2,1,0:T(8,128)(2,1)} async-done(((bf16[1,16,768]{2,1,0:T(8,128)(2,1)}), bf16[64,16,768]{2,1,0:T(8,128)(2,1)}) %all-gather.11.cloned.1.call-update) | async-done | bytes 1572880 | tf_op jit(solution)/shard_map/all_gather | solution.py:138
  471.2 1.5 concatenate.146
  475.8 6.6 fusion.88
  483.3 170.1 %all-reduce.11.cloned.1.call-done = (f32[16,49]{1,0:T(8,128)}, f32[16]{0:T(128)}, f32[128,64]{0,1:T(8,128)}, f32[64,128]{1,0:T(8,128)}) async-done(((f32[16,49]{1,0:T(8,128)}, f32[16]{0:T(128)}, f32[128,64]{0,1:T(8,128)}, f32[64,128]{1,0:T(8,128)}), (f32[16,49]{1,0:T(8,128)}, f32[16]{0:T(128)}, f32[128,64]{0,1:T(8,128)}, f32[64,128]{1,0:T(8,128)})) %all-reduce.11.cloned.1.call-update) | async-done | bytes 68752 | tf_op jit(solution)/shard_map/psum | solution.py:142
  (302 shorter events, 32.5 us)
Async XLA Ops:
  7.2 169.5 %copy-start = (bf16[64,128]{1,0:T(8,128)(2,1)S(1)}, bf16[64,128]{1,0:T(8,128)(2,1)}, u32[]{:S(2)}) copy-start(bf16[64,128]{1,0:T(8,128)(2,1)} %param.13) | copy-start | bytes 49156
  7.2 92.8 %all-gather.5.cloned.1.call-start = ((), (), s32[]{:S(2)}) async-start(), calls=%async_computation | async-start | bytes 1597440 | tf_op jit(solution)/shard_map/all_gather | solution.py:98
  10.6 164.6 %all-gather.7.cloned.1.call-start = ((), (), s32[]{:S(2)}) async-start(), calls=%async_computation.1 | async-start | bytes 1179648 | tf_op jit(solution)/shard_map/all_gather | solution.py:108
  11.1 92.5 %copy-start.9 = (f32[16]{0:T(128)}, f32[16]{0:T(128)S(1)}, u32[]{:S(2)}) copy-start(f32[16]{0:T(128)S(1)} %get-tuple-element.128) | copy-start | bytes 196
  11.1 92.6 %copy-start.11 = (f32[16]{0:T(128)}, f32[16]{0:T(128)S(1)}, u32[]{:S(2)}) copy-start(f32[16]{0:T(128)S(1)} %get-tuple-element.129) | copy-start | bytes 196
  11.2 92.6 %copy-start.13 = (f32[16]{0:T(128)}, f32[16]{0:T(128)S(1)}, u32[]{:S(2)}) copy-start(f32[16]{0:T(128)S(1)} %get-tuple-element.130) | copy-start | bytes 196
  11.2 92.6 %copy-start.15 = (f32[16]{0:T(128)}, f32[16]{0:T(128)S(1)}, u32[]{:S(2)}) copy-start(f32[16]{0:T(128)S(1)} %get-tuple-element.131) | copy-start | bytes 196
  11.7 92.1 %copy-start.17 = (f32[16]{0:T(128)}, f32[16]{0:T(128)S(1)}, u32[]{:S(2)}) copy-start(f32[16]{0:T(128)S(1)} %get-tuple-element.83) | copy-start | bytes 196
  11.7 92.1 %copy-start.19 = (f32[16]{0:T(128)}, f32[16]{0:T(128)S(1)}, u32[]{:S(2)}) copy-start(f32[16]{0:T(128)S(1)} %get-tuple-element.84) | copy-start | bytes 196
  11.7 92.1 %copy-start.21 = (f32[16]{0:T(128)}, f32[16]{0:T(128)S(1)}, u32[]{:S(2)}) copy-start(f32[16]{0:T(128)S(1)} %get-tuple-element.85) | copy-start | bytes 196
  11.7 92.1 %copy-start.23 = (f32[16]{0:T(128)}, f32[16]{0:T(128)S(1)}, u32[]{:S(2)}) copy-start(f32[16]{0:T(128)S(1)} %get-tuple-element.86) | copy-start | bytes 196
  11.7 92.1 %copy-start.25 = (f32[16]{0:T(128)}, f32[16]{0:T(128)S(1)}, u32[]{:S(2)}) copy-start(f32[16]{0:T(128)S(1)} %get-tuple-element.87) | copy-start | bytes 196
  11.7 92.1 %copy-start.27 = (f32[16]{0:T(128)}, f32[16]{0:T(128)S(1)}, u32[]{:S(2)}) copy-start(f32[16]{0:T(128)S(1)} %get-tuple-element.88) | copy-start | bytes 196
  11.7 92.1 %copy-start.29 = (f32[16]{0:T(128)}, f32[16]{0:T(128)S(1)}, u32[]{:S(2)}) copy-start(f32[16]{0:T(128)S(1)} %get-tuple-element.89) | copy-start | bytes 196
  11.7 92.1 %copy-start.31 = (f32[16]{0:T(128)}, f32[16]{0:T(128)S(1)}, u32[]{:S(2)}) copy-start(f32[16]{0:T(128)S(1)} %get-tuple-element.90) | copy-start | bytes 196
  11.7 92.1 %copy-start.33 = (f32[16]{0:T(128)}, f32[16]{0:T(128)S(1)}, u32[]{:S(2)}) copy-start(f32[16]{0:T(128)S(1)} %get-tuple-element.91) | copy-start | bytes 196
  11.8 92.1 %copy-start.35 = (f32[16]{0:T(128)}, f32[16]{0:T(128)S(1)}, u32[]{:S(2)}) copy-start(f32[16]{0:T(128)S(1)} %get-tuple-element.92) | copy-start | bytes 196
  11.8 92.1 %copy-start.37 = (f32[16]{0:T(128)}, f32[16]{0:T(128)S(1)}, u32[]{:S(2)}) copy-start(f32[16]{0:T(128)S(1)} %get-tuple-element.93) | copy-start | bytes 196
  11.8 92.1 %copy-start.39 = (f32[16]{0:T(128)}, f32[16]{0:T(128)S(1)}, u32[]{:S(2)}) copy-start(f32[16]{0:T(128)S(1)} %get-tuple-element.94) | copy-start | bytes 196
  135.8 82.3 %all-gather.9.cloned.1.call-start = ((), (), s32[]{:S(2)}) async-start(), calls=%async_computation.2 | async-start | bytes 1179648 | tf_op jit(solution)/shard_map/all_gather | solution.py:120
  136.6 212.3 %all-reduce.13.cloned.1.call-start = ((), (), s32[]{:S(2)}) async-start(), calls=%async_computation.5 | async-start | bytes 8388608
  230.4 143.1 %copy-start.4 = (bf16[1,16,4096]{2,1,0:T(8,128)(2,1)S(1)}, bf16[1,16,4096]{2,1,0:T(8,128)(2,1)}, u32[]{:S(2)}) copy-start(bf16[1,16,4096]{2,1,0:T(8,128)(2,1)} %param.8) | copy-start | bytes 393220
  230.5 240.8 %all-gather.11.cloned.1.call-start = ((), (), s32[]{:S(2)}) async-start(), calls=%async_computation.3 | async-start | bytes 1597440 | tf_op jit(solution)/shard_map/all_gather | solution.py:138
  382.2 271.2 %all-reduce.11.cloned.1.call-start = ((), (), s32[]{:S(2)}) async-start(), calls=%async_computation.4 | async-start | bytes 148480 | tf_op jit(solution)/shard_map/psum | solution.py:142
  (72 other events, 2402.6 us)
Sparse Core Ops, SparseCore 0:
  11.9 88.0 all-gather.4
  135.9 39.2 all-gather.6
  177.9 40.2 all-gather.8
  230.6 118.3 all-reduce.12
  382.3 88.8 all-gather.10
  475.5 177.8 all-reduce.10
where the time goes:
time: 666 us
  waiting for transfers between devices  524 us (79%)
  blocking collectives  44.9 us (7%)
  local copies, waits for them, and re-layouts  40.3 us (6%)
  other arithmetic  30.1 us (5%)
  between operations  16.4 us (2%)
  matrix products  9.38 us (1%)
    psum x1, waiting for transfers between devices, body(): lax.psum((grad_in, grad_out, grad_gain, grad_kernel), 'tile')  170 us
    unnamed x7, waiting for transfers between devices  117 us
    all_gather x1, waiting for transfers between devices, body(): table = lax.all_gather(rim_strips(grid), 'tile', axis=0, tiled=True)  86.9 us
    all_gather x1, waiting for transfers between devices, body(): dtable = lax.all_gather(rim_strips(dgrid), 'tile', axis=0, tiled=True)  72 us
    all_gather x1, waiting for transfers between devices, body(): masked = lax.all_gather(masked_mine, 'chan', axis=1, tiled=True)  39.9 us
    all_gather x1, waiting for transfers between devices, body(): feats = lax.all_gather(feats_mine, 'chan', axis=1, tiled=True)  38.5 us
    psum x1, blocking collectives, body(): lax.psum((jnp.sum(conv, 1), jnp.sum(conv * conv, 1)), 'chan')  23.7 us
    psum x1, blocking collectives, body(): lax.psum((jnp.sum(d_norm, 1), jnp.sum(d_norm * normed, 1)), 'chan')  21.3 us
  transfers between devices with their start and end apart: 6, of which 6 were waited for; matrix products, arithmetic and copies ran while one was open for 5% of the time, Pallas kernels for 0%

commit v1 on v0

v1 whole, which is shorter than its diff:
```python
import jax
import jax.numpy as jnp
from jax import lax
from jax.experimental import pallas as pl
from jax.experimental.pallas import tpu as pltpu
from jax.sharding import PartitionSpec as P

EPS = 1e-06
N = 8
F32 = jnp.float32
BF16 = jnp.bfloat16

(RIM_Y, RIM_X, DRIM_Y, DRIM_X, WEIGHTS, MASKED, CONV, MEANS, DCONV, BRANCH, GAIN, G_X, G_Z, G_Y, G_ALL, S_Y, S_X) = range(17)


def dot(a, b, dims):
    return lax.dot_general(a, b, (dims, ((), ())), preferred_element_type=F32)


def lanes(t, width=128):
    return pl.ds(pl.multiple_of(t * width, width), width)


def rows16(p):
    return pl.ds(pl.multiple_of(p * 16, 16), 16)


def kernel_body(
    act, cot, ker, gain, w_in, w_out, nbr, mask,
    out, igrad, small_out, wgrad_out,
    xpad, dpad, wb, rim, drim, table, dtable, masks, hsend, dhsend, hbuf, dhbuf,
    weights, masked, conv_r, means, convs, mean_all, dz, normed, feats, act_h, dpre_h,
    dconv_s, dconv, branch_s, branch, gain_s, gains, g_s, g_x, g_xs, g_z, g_y, g_all, s_y, s_x,
    ssem, rsem,
):
    tile = lax.axis_index("tile")
    z = lax.axis_index("chan")
    y = tile // N
    q = lax.rem(tile, N)
    mine = {"y": y, "x": q, "z": z}

    def device(group, p):
        if group == "y":
            return (p * N + q, z)
        if group == "x":
            return (y * N + p, z)
        return (tile, p)

    def copy(stage, group, src, dst, to, slot):
        return pltpu.make_async_remote_copy(
            src_ref=src,
            dst_ref=dst,
            send_sem=ssem.at[stage, to],
            recv_sem=rsem.at[stage, slot],
            device_id=device(group, to),
            device_id_type=pl.DeviceIdType.MESH,
        )

    def peers(group, step):
        def one(j, carry):
            step(lax.rem(mine[group] + j, N))
            return carry

        lax.fori_loop(1, N, one, 0)

    sent = []

    def start(stage, group, src, dst):
        me = mine[group]
        peers(group, lambda p: copy(stage, group, src(p), dst(me), p, me).start())
        sent.append((stage, group, src, dst))

    def arrive(stage, group, src, dst):
        peers(group, lambda p: copy(stage, group, src(p), dst(p), p, p).wait_recv())

    lane = lax.broadcasted_iota(jnp.int32, (16, 128), 1)
    lane1 = lax.broadcasted_iota(jnp.int32, (1, 1, 128), 2)
    low = lane < 64
    rest = lane & 63
    edge = (rest < 3) | (rest >= 61)
    beside = ((lane >= 64) & (lane < 67)) | (lane >= 125)

    def window_in(index, members):
        found = index < 0
        for member in members:
            found = found | (index == member)
        return found

    def pair(ref, t):
        return ref[:, lanes(t)].astype(F32)

    def roll(x, shift, axis):
        shift = shift % 128
        return x if shift == 0 else pltpu.roll(x, shift, axis)

    barrier = pltpu.get_barrier_semaphore()
    for group in ("y", "x", "z"):
        peers(
            group,
            lambda p, group=group: pl.semaphore_signal(
                barrier, inc=1, device_id=device(group, p), device_id_type=pl.DeviceIdType.MESH
            ),
        )

    def build_rim(src, dst):
        first = src[:, 0:128]
        dst[0:16, :] = first
        dst[16:32, :] = jnp.where(low, pair(src, 1), pair(src, 30)).astype(BF16)
        dst[32:48, :] = src[:, 3968:4096]

        def pack(block, carry):
            total = jnp.zeros((16, 128), F32)
            for t in range(8):
                total = total + roll(jnp.where(edge, pair(src, block * 8 + t), 0.0), 8 * t, 1)
            dst[rows16(3 + block), :] = total.astype(BF16)
            return carry

        lax.fori_loop(0, 4, pack, 0)

    build_rim(act, rim)
    list_row = lax.broadcasted_iota(jnp.int32, (16, 128), 0)
    listed = jnp.full((16, 128), -1.0, F32)
    for k in range(8):
        listed = jnp.where(list_row == k, nbr[0, k].astype(F32), listed)
    rim[112:128, :] = listed.astype(BF16)

    pl.semaphore_wait(barrier, 3 * (N - 1))
    rim_src, rim_dst = (lambda p: rim), (lambda p: table.at[p])
    start(RIM_Y, "y", rim_src, rim_dst)

    eye = (
        lax.broadcasted_iota(jnp.int32, (64, 64), 0) == lax.broadcasted_iota(jnp.int32, (64, 64), 1)
    ).astype(BF16)
    weights[z, 0:64, :] = dot(eye, w_in[...], ((1,), (1,))).astype(BF16)
    weights[z, 64:128, :] = w_out[...]
    w_src, w_dst = (lambda p: weights.at[z]), (lambda p: weights.at[p])
    start(WEIGHTS, "z", w_src, w_dst)

    def mask_cot(t, carry):
        kept = mask[:, lanes(t, 512)].astype(F32)
        masked[:, lanes(t, 512)] = (cot[:, lanes(t, 512)].astype(F32) * kept).astype(BF16)
        return carry

    lax.fori_loop(0, 8, mask_cot, 0)
    m_src, m_dst = (lambda p: masked.at[:, lanes(p, 512)]), (lambda p: dz.at[rows16(p), :])
    start(MASKED, "z", m_src, m_dst)
    dz[rows16(z), :] = masked[:, lanes(z, 512)]

    for tap in range(49):
        wb[tap] = jnp.broadcast_to(ker[:, tap : tap + 1], (16, 128))

    def spread(src, dst):
        def rows(t, carry):
            both = pair(src, t)
            dst[3 + 2 * t] = jnp.where(low, both, 0.0)
            dst[4 + 2 * t] = jnp.where(low, roll(both, 64, 1), 0.0)
            return carry

        lax.fori_loop(0, 32, rows, 0)

    spread(act, xpad)

    index4 = lane1 // 4
    odd = (index4 & 1) == 1
    in_top = window_in(index4, (0, 15, 16, 31, 2, 17))
    in_bottom = window_in(index4, (28, 11, 14, 29, 30, 13))
    table_own = table.at[y]
    table_own[...] = rim[...]
    arrive(RIM_Y, "y", rim_src, rim_dst)

    def make_masks(d, carry):
        number = (y * N + d).astype(F32)
        near = (table[:, 112:128, :].astype(F32) == number).astype(F32)
        m = [near[:, k : k + 1, :] for k in range(8)]
        masks[d, :, 0:1, :] = m[1]
        masks[d, :, 1:2, :] = jnp.where(lane1 < 64, m[1], m[6])
        masks[d, :, 2:3, :] = m[6]
        masks[d, :, 3:4, :] = jnp.where(odd, m[4], m[3])
        masks[d, :, 4:5, :] = jnp.where(
            in_top, jnp.where(odd, m[2], m[0]), jnp.where(in_bottom, jnp.where(odd, m[7], m[5]), 0.0)
        )
        return carry

    lax.fori_loop(0, N, make_masks, 0)

    def choose(src, dst):
        def one(d, carry):
            for part in range(8):
                if part < 7:
                    block = src[:, 16 * part : 16 * part + 16, :].astype(F32)
                else:
                    block = jnp.where(
                        in_bottom, src[:, 96:112, :].astype(F32), src[:, 48:64, :].astype(F32)
                    )
                kind = part if part < 3 else 3 if part < 7 else 4
                total = jnp.sum(masks[d, :, kind : kind + 1, :] * block, 0)
                dst[d, 16 * part : 16 * part + 16, :] = total.astype(BF16)
            return carry

        lax.fori_loop(0, N, one, 0)

    def finish_halo(own, got, dst):
        def part(i):
            total = own[q, 16 * i : 16 * i + 16, :].astype(F32)
            for j in range(1, N):
                total = total + got[lax.rem(q + j, N), 16 * i : 16 * i + 16, :].astype(F32)
            return total

        top, mid, end, corner = part(0), part(1), part(2), part(7)

        def outer(row, center, shift):
            dst[row] = jnp.where(low, center, jnp.where(beside, roll(corner, shift, 1), 0.0))

        outer(67, top, 64)
        outer(68, roll(top, 64, 1), 0)
        outer(69, mid, 56)
        outer(0, roll(mid, 64, 1), 80)
        outer(1, end, 8)
        outer(2, roll(end, 64, 1), 72)
        for block in range(4):
            cols = part(3 + block)
            for t in range(8):
                for o in range(2):
                    row = 3 + 16 * block + 2 * t + o
                    near = roll(cols, 64 * (1 - o) - 8 * t, 1)
                    dst[row] = dst[row] + jnp.where(beside, near, 0.0)

    choose(table, hsend)
    h_src, h_dst = (lambda p: hsend.at[p]), (lambda p: hbuf.at[p])
    start(RIM_X, "x", h_src, h_dst)
    arrive(RIM_X, "x", h_src, h_dst)
    finish_halo(hsend, hbuf, xpad)

    def filtered(src, flip, r):
        total = None
        for b in range(7):
            part = None
            for a in range(7):
                tap = (6 - a) * 7 + 6 - b if flip else a * 7 + b
                term = wb[tap][None] * src[pl.ds(8 * r + a, 8)]
                part = term if part is None else part + term
            part = roll(part, 3 - b, 2)
            total = part if total is None else total + part
        return [jnp.where(low, total[2 * u], roll(total[2 * u + 1], 64, 1)) for u in range(4)]

    c_src, c_dst = (lambda p: conv_r.at[:, lanes(p, 512)]), (lambda p: convs.at[rows16(p), :])
    a_src, a_dst = (lambda p: means.at[:, lanes(p, 512)]), (lambda p: mean_all.at[p])

    def forward(j, carry):
        r = lax.rem(z + 1 + j, N)
        tiles = filtered(xpad, False, r)
        for u in range(4):
            mean = jnp.sum(tiles[u], 0, keepdims=True) * (1.0 / 16)
            conv_r[:, lanes(4 * r + u)] = (tiles[u] - mean).astype(BF16)
            means[:, lanes(4 * r + u)] = mean

        @pl.when(j < N - 1)
        def _():
            copy(CONV, "z", c_src(r), c_dst(z), r, z).start()
            copy(MEANS, "z", a_src(r), a_dst(z), r, z).start()

        return carry

    lax.fori_loop(0, N, forward, 0)
    sent.append((CONV, "z", c_src, c_dst))
    sent.append((MEANS, "z", a_src, a_dst))
    convs[rows16(z), :] = conv_r[:, lanes(z, 512)]
    mean_all[z] = means[:, lanes(z, 512)]
    arrive(CONV, "z", c_src, c_dst)
    arrive(MEANS, "z", a_src, a_dst)

    local = mean_all[...]
    mean = jnp.sum(local, 0) * (1.0 / N)
    centred = (convs[...].astype(F32).reshape(N, 16, 512) + (local - mean[None])).reshape(128, 512)
    rstd = lax.rsqrt(jnp.sum(centred * centred, 0, keepdims=True) * (1.0 / 128) + EPS)
    normed[...] = centred * rstd
    diagonal = lax.broadcasted_iota(jnp.int32, (128, 128), 0) == lax.broadcasted_iota(
        jnp.int32, (128, 128), 1
    )
    gain_col = jnp.sum(jnp.where(diagonal, jnp.broadcast_to(gain[...], (128, 128)), 0.0), 1, keepdims=True)
    feats[...] = (normed[...] * gain_col).astype(BF16)
    arrive(WEIGHTS, "z", w_src, w_dst)
    arrive(MASKED, "z", m_src, m_dst)

    def hidden(g, carry):
        wi = weights[pl.ds(2 * g, 2), 0:64, :].reshape(128, 128)
        wo = weights[pl.ds(2 * g, 2), 64:128, :].reshape(128, 128)
        pre = dot(wi, feats[...], ((1,), (0,)))
        square = pre * pre
        bend = jnp.tanh(0.7978845608 * pre * (1.0 + 0.044715 * square))
        half = 0.5 + 0.5 * bend
        act_h[lanes(g), :] = (pre * half).astype(BF16)
        slope = half + (0.5 * 0.7978845608) * pre * (1.0 - bend * bend) * (
            1.0 + (3.0 * 0.044715) * square
        )
        d_act = dot(wo, dz[...], ((1,), (0,)))
        dpre_h[lanes(g), :] = (d_act * slope).astype(BF16)
        return carry

    lax.fori_loop(0, 4, hidden, 0)
    wi_all = weights[:, 0:64, :].reshape(512, 128)
    wo_all = weights[:, 64:128, :].reshape(512, 128)
    d_feat = dot(wi_all, dpre_h[...], ((0,), (0,)))
    per_gain = d_feat * normed[...]
    d_norm = d_feat * gain_col
    first = jnp.sum(d_norm, 0, keepdims=True) * (1.0 / 128)
    second = jnp.sum(per_gain * gain_col, 0, keepdims=True) * (1.0 / 128)
    dconv_s[...] = (rstd * (d_norm - first - normed[...] * second)).astype(BF16)
    d_src, d_dst = (lambda p: dconv_s.at[rows16(p), :]), (lambda p: dconv.at[:, lanes(p, 512)])
    start(DCONV, "z", d_src, d_dst)
    dconv[:, lanes(z, 512)] = dconv_s[rows16(z), :]
    folded = per_gain[:, 0:128] + per_gain[:, 128:256] + per_gain[:, 256:384] + per_gain[:, 384:512]
    gain_s[...] = folded.reshape(N, 16, 128)
    n_src, n_dst = (lambda p: gain_s.at[p]), (lambda p: gains.at[p])
    start(GAIN, "z", n_src, n_dst)
    gains[z] = gain_s[z]

    g_s[:, 0:64, :] = dot(dpre_h[...], feats[...], ((1,), (1,))).astype(BF16).reshape(N, 64, 128)
    g_s[:, 64:128, :] = dot(act_h[...], dz[...], ((1,), (1,))).astype(BF16).reshape(N, 64, 128)
    gx_src, gx_dst = (lambda p: g_s.at[:, rows16(p), :]), (lambda p: g_x.at[p])
    start(G_X, "x", gx_src, gx_dst)
    branch_s[...] = dot(wo_all, act_h[...], ((0,), (0,))).astype(BF16)
    b_src, b_dst = (lambda p: branch_s.at[rows16(p), :]), (lambda p: branch.at[:, lanes(p, 512)])
    start(BRANCH, "z", b_src, b_dst)
    branch[:, lanes(z, 512)] = branch_s[rows16(z), :]

    arrive(DCONV, "z", d_src, d_dst)
    build_rim(dconv, drim)
    e_src, e_dst = (lambda p: drim), (lambda p: dtable.at[p])
    start(DRIM_Y, "y", e_src, e_dst)
    dtable[y] = drim[...]
    spread(dconv, dpad)

    arrive(G_X, "x", gx_src, gx_dst)
    g_x[q] = g_s[:, rows16(q), :]
    g_xs[...] = jnp.sum(g_x[...].astype(F32), 0)
    gz_src, gz_dst = (lambda p: g_xs.at[p]), (lambda p: g_z.at[p])
    start(G_Z, "z", gz_src, gz_dst)
    g_z[z] = g_xs[z]

    small = jnp.zeros((16, 128), F32)
    for b in range(7):

        def taps(r, carry, b=b):
            moved = roll(dpad[pl.ds(3 + 8 * r, 8)], b - 3, 2)
            return tuple(
                carry[a] + jnp.sum(moved * xpad[pl.ds(8 * r + a, 8)], 0) for a in range(7)
            )

        column = lax.fori_loop(0, 8, taps, tuple(jnp.zeros((16, 128), F32) for _ in range(7)))
        for a in range(7):
            small = jnp.where(lane == a * 7 + b, jnp.sum(column[a], 1, keepdims=True), small)
    arrive(GAIN, "z", n_src, n_dst)
    small = jnp.where(lane == 49, jnp.sum(jnp.sum(gains[...], 0), 1, keepdims=True), small)
    s_y[y] = small
    sy_src, sy_dst = (lambda p: s_y.at[y]), (lambda p: s_y.at[p])
    start(S_Y, "y", sy_src, sy_dst)

    arrive(DRIM_Y, "y", e_src, e_dst)
    choose(dtable, dhsend)
    f_src, f_dst = (lambda p: dhsend.at[p]), (lambda p: dhbuf.at[p])
    start(DRIM_X, "x", f_src, f_dst)

    arrive(G_Z, "z", gz_src, gz_dst)
    g_y[y] = jnp.sum(g_z[...], 0)
    gy_src, gy_dst = (lambda p: g_y.at[y]), (lambda p: g_y.at[p])
    start(G_Y, "y", gy_src, gy_dst)

    arrive(BRANCH, "z", b_src, b_dst)

    def write_out(t, carry):
        at = lanes(t, 512)
        kept = mask[:, at].astype(F32)
        out[:, at] = (act[:, at].astype(F32) + kept * branch[:, at].astype(F32)).astype(BF16)
        return carry

    lax.fori_loop(0, 8, write_out, 0)

    arrive(S_Y, "y", sy_src, sy_dst)
    s_x[q] = jnp.sum(s_y[...], 0)
    sx_src, sx_dst = (lambda p: s_x.at[q]), (lambda p: s_x.at[p])
    start(S_X, "x", sx_src, sx_dst)
    arrive(G_Y, "y", gy_src, gy_dst)
    g_all[q] = jnp.sum(g_y[...], 0)
    ga_src, ga_dst = (lambda p: g_all.at[q]), (lambda p: g_all.at[p])
    start(G_ALL, "x", ga_src, ga_dst)

    arrive(DRIM_X, "x", f_src, f_dst)
    finish_halo(dhsend, dhbuf, dpad)

    def backward(r, carry):
        tiles = filtered(dpad, True, r)
        for u in range(4):
            at = lanes(4 * r + u)
            igrad[:, at] = (cot[:, at].astype(F32) + tiles[u]).astype(BF16)
        return carry

    lax.fori_loop(0, N, backward, 0)

    arrive(S_X, "x", sx_src, sx_dst)
    small_out[...] = jnp.sum(s_x[...], 0)
    arrive(G_ALL, "x", ga_src, ga_dst)
    wgrad_out[...] = g_all[...].reshape(128, 128)
    for stage, group, src, dst in sent:
        me = mine[group]
        peers(group, lambda p: copy(stage, group, src(p), dst(me), p, me).wait_send())


def body(activations, cotangent, kernel, gain, w_in, w_out, neighbours, land_mask):
    vmem = pl.BlockSpec(memory_space=pltpu.VMEM)
    smem = pl.BlockSpec(memory_space=pltpu.SMEM)
    scratch = [
        ((70, 16, 128), F32),
        ((70, 16, 128), F32),
        ((49, 16, 128), F32),
        ((128, 128), BF16),
        ((128, 128), BF16),
        ((N, 128, 128), BF16),
        ((N, 128, 128), BF16),
        ((N, N, 8, 128), F32),
        ((N, 128, 128), BF16),
        ((N, 128, 128), BF16),
        ((N, 128, 128), BF16),
        ((N, 128, 128), BF16),
        ((N, 128, 128), BF16),
        ((16, 4096), BF16),
        ((16, 4096), BF16),
        ((1, 4096), F32),
        ((128, 512), BF16),
        ((N, 1, 512), F32),
        ((128, 512), BF16),
        ((128, 512), F32),
        ((128, 512), BF16),
        ((512, 512), BF16),
        ((512, 512), BF16),
        ((128, 512), BF16),
        ((16, 4096), BF16),
        ((128, 512), BF16),
        ((16, 4096), BF16),
        ((N, 16, 128), F32),
        ((N, 16, 128), F32),
        ((N, 128, 128), BF16),
        ((N, N, 16, 128), BF16),
        ((N, 16, 128), F32),
        ((N, 16, 128), F32),
        ((N, 16, 128), F32),
        ((N, 16, 128), F32),
        ((N, 16, 128), F32),
        ((N, 16, 128), F32),
    ]
    out, igrad, small, wgrad = pl.pallas_call(
        kernel_body,
        out_shape=(
            jax.ShapeDtypeStruct((16, 4096), BF16),
            jax.ShapeDtypeStruct((16, 4096), BF16),
            jax.ShapeDtypeStruct((16, 128), F32),
            jax.ShapeDtypeStruct((128, 128), F32),
        ),
        in_specs=[vmem, vmem, vmem, vmem, vmem, vmem, smem, vmem],
        out_specs=[vmem] * 4,
        scratch_shapes=[pltpu.VMEM(shape, kind) for shape, kind in scratch]
        + [pltpu.SemaphoreType.DMA((17, N)), pltpu.SemaphoreType.DMA((17, N))],
        compiler_params=pltpu.CompilerParams(
            collective_id=0, has_side_effects=True, vmem_limit_bytes=40 * 1024 * 1024
        ),
        cost_estimate=pl.CostEstimate(flops=360000000, bytes_accessed=1000000, transcendentals=262144),
        name="block",
    )(
        activations[0], cotangent[0], kernel, gain.reshape(1, 128), w_in, w_out, neighbours, land_mask,
    )
    return (
        out[None],
        igrad[None],
        small[:, :49],
        small[:, 49],
        wgrad[:64].T,
        wgrad[64:],
    )


def solution(mesh):
    placed = (
        P("tile", "chan", None),
        P("tile", "chan", None),
        P("chan", None),
        P(),
        P(None, "chan"),
        P("chan", None),
        P("tile", None),
        P("tile", None),
    )
    return jax.shard_map(
        body,
        mesh=mesh,
        in_specs=placed,
        out_specs=(
            P("tile", "chan", None),
            P("tile", "chan", None),
            P("chan", None),
            P("chan"),
            P(None, "chan"),
            P("chan", None),
        ),
        check_vma=False,
    )
```

time: 666 us -> 74.6 us (0.11)
  waiting for transfers between devices: 524 us -> 0 us
  Pallas kernels: 0 us -> 67.8 us
  blocking collectives: 44.9 us -> 0 us
  local copies, waits for them, and re-layouts: 40.3 us -> 5.91 us
  other arithmetic: 30.1 us -> 0 us
  between operations: 16.4 us -> 0.73 us
  matrix products: 9.38 us -> 0 us
    all_gather x4 -> x0, waiting for transfers between devices: 237 us -> none  [the longest x1 86.9 us: body(): table = lax.all_gather(rim_strips(grid), 'tile', axis=0, tiled=True)]
    psum x1 -> x0, waiting for transfers between devices: 170 us -> none  [body(): lax.psum((grad_in, grad_out, grad_gain, grad_kernel), 'tile')]
    unnamed x7 -> x0, waiting for transfers between devices: 117 us -> none
    pallas_call x0 -> x1, Pallas kernels: none -> 67.8 us  [body(): pl.pallas_call(kernel_body, out_shape=(jax.ShapeDtypeStruct((16, 4096), B...]
    psum x2 -> x0, blocking collectives: 44.9 us -> none  [the longest x1 23.7 us: body(): lax.psum((jnp.sum(conv, 1), jnp.sum(conv * conv, 1)), 'chan')]
    reduce_sum x6 -> x0, other arithmetic: 17.4 us -> none  [the longest x4 9.65 us: kernel_grad_of(): jnp.sum(weights * padded[:, :, row:row + side, col:col + side].astype(jnp...]
    convert_element_type x2 -> x0, local copies, waits for them, and re-layouts: 9.73 us -> none  [the longest x1 5.49 us: body(): terms.astype(jnp.bfloat16)]
    dot_general x6 -> x0, matrix products: 9.38 us -> none  [the longest x1 2.67 us: body(): jnp.einsum('thp,tcp->hc', act, masked, preferred_element_type=jnp.float32)]
  transfers between devices with their start and end apart: 6 -> 0, of which waited for: 6 -> 0; matrix products, arithmetic and copies ran while one was open for 5% -> 0% of each run, Pallas kernels for 0% -> 0%
where the time goes in v1:
time: 74.6 us; the launch traced here: 74.4 us
  Pallas kernels  67.8 us (91%)
  local copies, waits for them, and re-layouts  5.91 us (8%)
    pallas_call x1, Pallas kernels, body(): pl.pallas_call(kernel_body, out_shape=(jax.ShapeDtypeStruct((16, 4096), B...  67.8 us
    unnamed x18, local copies, waits for them, and re-layouts  4.58 us

profile of v1, /device:TPU:1, one launch (start us, length us, event | category | flops | bytes accessed | tf_op | source)
XLA Modules:
  0.0 74.4 jit_solution(9743918594530731561)
XLA Ops:
  0.6 0.0 copy-start.2
  0.6 0.0 copy-start.3
  0.7 0.0 copy-start.4
  0.7 0.0 copy-start.5
  0.7 0.0 copy-start.6
  0.7 0.9 %copy.15.w_in = bf16[128,64]{1,0:T(8,128)(2,1)S(1)} copy(bf16[128,64]{0,1:T(8,128)(2,1)} %param.12) | data formatting | bytes 32768 | tf_op args[4]
  1.5 0.0 copy-done.2
  1.5 0.0 copy-done.3
  1.6 0.0 copy-done.4
  1.6 0.0 copy-done.5
  1.6 0.0 copy-done.6
  1.6 0.0 copy-start
  1.6 0.9 %copy-done = bf16[1,16,4096]{2,1,0:T(8,128)(2,1)S(1)} copy-done((bf16[1,16,4096]{2,1,0:T(8,128)(2,1)S(1)}, bf16[1,16,4096]{2,1,0:T(8,128)(2,1)}, u32[]{:S(2)}) %copy-start) | copy-done | bytes 131096
  2.5 0.0 copy-start.1
  2.5 0.9 %copy-done.1 = bf16[1,16,4096]{2,1,0:T(8,128)(2,1)S(1)} copy-done((bf16[1,16,4096]{2,1,0:T(8,128)(2,1)S(1)}, bf16[1,16,4096]{2,1,0:T(8,128)(2,1)}, u32[]{:S(2)}) %copy-start.1) | copy-done | bytes 131096
  3.4 67.8 %block.1 = (bf16[16,4096]{1,0:T(8,128)(2,1)S(1)}, bf16[16,4096]{1,0:T(8,128)(2,1)S(1)}, f32[16,128]{1,0:T(8,128)S(1)}, f32[128,128]{1,0:T(8,128)S(1)}) custom-call(bf16[16,4096]{1,0:T(8,128)(2,1)S(1)} %bitcast.11, bf16[16,4096]{1,0:T(8,128)(2,1)S(1)} %bitcast.12, f32[16,49]{1,0:T(8,128)S(1)} %copy-done.4, f32[1,128]{1,0:T(1,128)S(1)} %bitcast.13, ...), custom_call_target="tpu_custom_call" | custom-call | flops 360000000 | bytes 1000000 | tf_op jit(solution)/shard_map/block/pallas_call | solution.py:451
  71.2 0.7 slice_reduce_fusion
  71.9 0.6 fusion
  72.5 0.7 copy.19
  73.2 0.7 copy.20
  73.8 0.6 copy.21
Async XLA Ops:
  0.6 0.9 %copy-start.2 = (bf16[64,128]{1,0:T(8,128)(2,1)S(1)}, bf16[64,128]{1,0:T(8,128)(2,1)}, u32[]{:S(2)}) copy-start(bf16[64,128]{1,0:T(8,128)(2,1)} %w_out.1) | copy-start | bytes 49156
  0.6 0.9 %copy-start.3 = (s32[1,4096]{1,0:T(1,128)S(1)}, s32[1,4096]{1,0:T(1,128)}, u32[]{:S(2)}) copy-start(s32[1,4096]{1,0:T(1,128)} %mask.1) | copy-start | bytes 49156
  0.7 0.9 %copy-start.4 = (f32[16,49]{1,0:T(8,128)S(1)}, f32[16,49]{1,0:T(8,128)}, u32[]{:S(2)}) copy-start(f32[16,49]{1,0:T(8,128)} %ker.1) | copy-start | bytes 9412
  0.7 0.9 %copy-start.5 = (f32[128]{0:T(128)S(1)}, f32[128]{0:T(128)}, u32[]{:S(2)}) copy-start(f32[128]{0:T(128)} %param.11) | copy-start | bytes 1540
  0.7 0.9 %copy-start.6 = (s32[1,8]{1,0:T(1,128)S(1)}, s32[1,8]{1,0:T(1,128)}, u32[]{:S(2)}) copy-start(s32[1,8]{1,0:T(1,128)} %nbr.1) | copy-start | bytes 100
  1.6 0.9 %copy-start = (bf16[1,16,4096]{2,1,0:T(8,128)(2,1)S(1)}, bf16[1,16,4096]{2,1,0:T(8,128)(2,1)}, u32[]{:S(2)}) copy-start(bf16[1,16,4096]{2,1,0:T(8,128)(2,1)} %param.8) | copy-start | bytes 393220
  2.5 0.9 %copy-start.1 = (bf16[1,16,4096]{2,1,0:T(8,128)(2,1)S(1)}, bf16[1,16,4096]{2,1,0:T(8,128)(2,1)}, u32[]{:S(2)}) copy-start(bf16[1,16,4096]{2,1,0:T(8,128)(2,1)} %param.9) | copy-start | bytes 393220

commit v2 on v1

--- a/solution.py
+++ b/solution.py
@@ -9,8 +9,12 @@
 N = 8
 F32 = jnp.float32
 BF16 = jnp.bfloat16
-
-(RIM_Y, RIM_X, DRIM_Y, DRIM_X, WEIGHTS, MASKED, CONV, MEANS, DCONV, BRANCH, GAIN, G_X, G_Z, G_Y, G_ALL, S_Y, S_X) = range(17)
+VMEM_LIMIT = 60 * 1024 * 1024
+
+(
+    ROWS_X, COLS_Y, ROWS_Y, COLS_X, D_ROWS_X, D_COLS_Y, D_ROWS_Y, D_COLS_X,
+    WEIGHTS, MASKED, CONV, MEANS, DCONV, BRANCH, GAIN, G_X, G_Z, G_Y, G_ALL, S_Y, S_X,
+) = range(21)
 
 
 def dot(a, b, dims):
@@ -26,12 +30,16 @@
 
 
 def kernel_body(
+    act_h, cot_h, ker_h, gain_h, w_in_h, w_out_h, nbr_h, mask_h,
+    out_h, igrad_h, kgrad_h, ggrad_h, w_in_grad_h, w_out_grad_h,
     act, cot, ker, gain, w_in, w_out, nbr, mask,
-    out, igrad, small_out, wgrad_out,
-    xpad, dpad, wb, rim, drim, table, dtable, masks, hsend, dhsend, hbuf, dhbuf,
-    weights, masked, conv_r, means, convs, mean_all, dz, normed, feats, act_h, dpre_h,
+    out, igrad, kgrad_out, gain_out, w_in_out, w_out_out,
+    xpad, dpad, wb, rows, cols, d_rows, d_cols,
+    rows_t, cols_t, d_rows_t, d_cols_t, row_masks, col_masks,
+    rows_s, cols_s, d_rows_s, d_cols_s, rows_g, cols_g, d_rows_g, d_cols_g,
+    weights, masked, conv_r, means, convs, mean_all, dz, normed, feats, act_h2, dpre_h,
     dconv_s, dconv, branch_s, branch, gain_s, gains, g_s, g_x, g_xs, g_z, g_y, g_all, s_y, s_x,
-    ssem, rsem,
+    ssem, rsem, lsem, osem,
 ):
     tile = lax.axis_index("tile")
     z = lax.axis_index("chan")
@@ -93,6 +101,19 @@
         shift = shift % 128
         return x if shift == 0 else pltpu.roll(x, shift, axis)
 
+    inputs = [
+        (act_h, act), (nbr_h, nbr), (cot_h, cot), (mask_h, mask),
+        (w_in_h, w_in), (w_out_h, w_out), (ker_h, ker), (gain_h, gain),
+    ]
+    loads = [pltpu.make_async_copy(src, dst, lsem.at[i]) for i, (src, dst) in enumerate(inputs)]
+    for load in loads:
+        load.start()
+    results = [
+        (out, out_h), (igrad, igrad_h), (kgrad_out, kgrad_h), (gain_out, ggrad_h),
+        (w_in_out, w_in_grad_h), (w_out_out, w_out_grad_h),
+    ]
+    stores = [pltpu.make_async_copy(src, dst, osem.at[i]) for i, (src, dst) in enumerate(results)]
+
     barrier = pltpu.get_barrier_semaphore()
     for group in ("y", "x", "z"):
         peers(
@@ -102,36 +123,44 @@
             ),
         )
 
-    def build_rim(src, dst):
-        first = src[:, 0:128]
-        dst[0:16, :] = first
+    def build_rows(src, dst):
+        dst[0:16, :] = src[:, 0:128]
         dst[16:32, :] = jnp.where(low, pair(src, 1), pair(src, 30)).astype(BF16)
         dst[32:48, :] = src[:, 3968:4096]
 
+    def build_cols(src, dst):
         def pack(block, carry):
             total = jnp.zeros((16, 128), F32)
             for t in range(8):
                 total = total + roll(jnp.where(edge, pair(src, block * 8 + t), 0.0), 8 * t, 1)
-            dst[rows16(3 + block), :] = total.astype(BF16)
+            dst[rows16(block), :] = total.astype(BF16)
             return carry
 
         lax.fori_loop(0, 4, pack, 0)
 
-    build_rim(act, rim)
-    list_row = lax.broadcasted_iota(jnp.int32, (16, 128), 0)
-    listed = jnp.full((16, 128), -1.0, F32)
-    for k in range(8):
-        listed = jnp.where(list_row == k, nbr[0, k].astype(F32), listed)
-    rim[112:128, :] = listed.astype(BF16)
+    loads[0].wait()
+    build_cols(act, cols)
+    build_rows(act, rows)
+    loads[1].wait()
+    eight = lax.broadcasted_iota(jnp.int32, (16, 8), 0) == lax.broadcasted_iota(jnp.int32, (16, 8), 1)
+    listed = jnp.sum(
+        jnp.where(eight, jnp.broadcast_to(nbr[...].astype(F32), (16, 8)), 0.0), 1, keepdims=True
+    )
+    listed = jnp.broadcast_to(listed, (16, 128)).astype(BF16)
+    rows[48:64, :] = listed
+    cols[64:80, :] = listed
 
     pl.semaphore_wait(barrier, 3 * (N - 1))
-    rim_src, rim_dst = (lambda p: rim), (lambda p: table.at[p])
-    start(RIM_Y, "y", rim_src, rim_dst)
-
-    eye = (
-        lax.broadcasted_iota(jnp.int32, (64, 64), 0) == lax.broadcasted_iota(jnp.int32, (64, 64), 1)
-    ).astype(BF16)
-    weights[z, 0:64, :] = dot(eye, w_in[...], ((1,), (1,))).astype(BF16)
+    c1_src, c1_dst = (lambda p: cols), (lambda p: cols_t.at[p])
+    start(COLS_Y, "y", c1_src, c1_dst)
+    r1_src, r1_dst = (lambda p: rows), (lambda p: rows_t.at[p])
+    start(ROWS_X, "x", r1_src, r1_dst)
+    cols_t[y] = cols[...]
+    rows_t[q] = rows[...]
+
+    for load in loads[2:]:
+        load.wait()
+    weights[z, 0:64, :] = w_in[...]
     weights[z, 64:128, :] = w_out[...]
     w_src, w_dst = (lambda p: weights.at[z]), (lambda p: weights.at[p])
     start(WEIGHTS, "z", w_src, w_dst)
@@ -164,49 +193,57 @@
     odd = (index4 & 1) == 1
     in_top = window_in(index4, (0, 15, 16, 31, 2, 17))
     in_bottom = window_in(index4, (28, 11, 14, 29, 30, 13))
-    table_own = table.at[y]
-    table_own[...] = rim[...]
-    arrive(RIM_Y, "y", rim_src, rim_dst)
-
-    def make_masks(d, carry):
-        number = (y * N + d).astype(F32)
-        near = (table[:, 112:128, :].astype(F32) == number).astype(F32)
-        m = [near[:, k : k + 1, :] for k in range(8)]
-        masks[d, :, 0:1, :] = m[1]
-        masks[d, :, 1:2, :] = jnp.where(lane1 < 64, m[1], m[6])
-        masks[d, :, 2:3, :] = m[6]
-        masks[d, :, 3:4, :] = jnp.where(odd, m[4], m[3])
-        masks[d, :, 4:5, :] = jnp.where(
+
+    def listed_as(table, first, number):
+        near = (table[:, first : first + 16, :].astype(F32) == number.astype(F32)).astype(F32)
+        return [near[:, k : k + 1, :] for k in range(8)]
+
+    def make_col_masks(d, carry):
+        m = listed_as(cols_t, 64, y * N + d)
+        col_masks[d, :, 0:1, :] = jnp.where(odd, m[4], m[3])
+        col_masks[d, :, 1:2, :] = jnp.where(
             in_top, jnp.where(odd, m[2], m[0]), jnp.where(in_bottom, jnp.where(odd, m[7], m[5]), 0.0)
         )
         return carry
 
-    lax.fori_loop(0, N, make_masks, 0)
-
-    def choose(src, dst):
+    def make_row_masks(d, carry):
+        m = listed_as(rows_t, 48, d * N + q)
+        row_masks[d, :, 0:1, :] = m[1]
+        row_masks[d, :, 1:2, :] = jnp.where(lane1 < 64, m[1], m[6])
+        row_masks[d, :, 2:3, :] = m[6]
+        return carry
+
+    def choose_rows(src, dst):
         def one(d, carry):
-            for part in range(8):
-                if part < 7:
-                    block = src[:, 16 * part : 16 * part + 16, :].astype(F32)
-                else:
-                    block = jnp.where(
-                        in_bottom, src[:, 96:112, :].astype(F32), src[:, 48:64, :].astype(F32)
-                    )
-                kind = part if part < 3 else 3 if part < 7 else 4
-                total = jnp.sum(masks[d, :, kind : kind + 1, :] * block, 0)
+            for part in range(3):
+                block = src[:, 16 * part : 16 * part + 16, :].astype(F32)
+                total = jnp.sum(row_masks[d, :, part : part + 1, :] * block, 0)
                 dst[d, 16 * part : 16 * part + 16, :] = total.astype(BF16)
             return carry
 
         lax.fori_loop(0, N, one, 0)
 
-    def finish_halo(own, got, dst):
-        def part(i):
-            total = own[q, 16 * i : 16 * i + 16, :].astype(F32)
-            for j in range(1, N):
-                total = total + got[lax.rem(q + j, N), 16 * i : 16 * i + 16, :].astype(F32)
-            return total
-
-        top, mid, end, corner = part(0), part(1), part(2), part(7)
+    def choose_cols(src, dst):
+        def one(d, carry):
+            for part in range(4):
+                block = src[:, 16 * part : 16 * part + 16, :].astype(F32)
+                total = jnp.sum(col_masks[d, :, 0:1, :] * block, 0)
+                dst[d, 16 * part : 16 * part + 16, :] = total.astype(BF16)
+            block = jnp.where(in_bottom, src[:, 48:64, :].astype(F32), src[:, 0:16, :].astype(F32))
+            dst[d, 64:80, :] = jnp.sum(col_masks[d, :, 1:2, :] * block, 0).astype(BF16)
+            return carry
+
+        lax.fori_loop(0, N, one, 0)
+
+    def added(me, own, got, i):
+        total = own[me, 16 * i : 16 * i + 16, :].astype(F32)
+        for j in range(1, N):
+            total = total + got[lax.rem(me + j, N), 16 * i : 16 * i + 16, :].astype(F32)
+        return total
+
+    def finish_halo(own_rows, got_rows, own_cols, got_cols, dst):
+        top, mid, end = [added(y, own_rows, got_rows, i) for i in range(3)]
+        corner = added(q, own_cols, got_cols, 4)
 
         def outer(row, center, shift):
             dst[row] = jnp.where(low, center, jnp.where(beside, roll(corner, shift, 1), 0.0))
@@ -218,18 +255,26 @@
         outer(1, end, 8)
         outer(2, roll(end, 64, 1), 72)
         for block in range(4):
-            cols = part(3 + block)
+            side = added(q, own_cols, got_cols, block)
             for t in range(8):
                 for o in range(2):
                     row = 3 + 16 * block + 2 * t + o
-                    near = roll(cols, 64 * (1 - o) - 8 * t, 1)
+                    near = roll(side, 64 * (1 - o) - 8 * t, 1)
                     dst[row] = dst[row] + jnp.where(beside, near, 0.0)
 
-    choose(table, hsend)
-    h_src, h_dst = (lambda p: hsend.at[p]), (lambda p: hbuf.at[p])
-    start(RIM_X, "x", h_src, h_dst)
-    arrive(RIM_X, "x", h_src, h_dst)
-    finish_halo(hsend, hbuf, xpad)
+    arrive(ROWS_X, "x", r1_src, r1_dst)
+    lax.fori_loop(0, N, make_row_masks, 0)
+    choose_rows(rows_t, rows_s)
+    r2_src, r2_dst = (lambda p: rows_s.at[p]), (lambda p: rows_g.at[p])
+    start(ROWS_Y, "y", r2_src, r2_dst)
+    arrive(COLS_Y, "y", c1_src, c1_dst)
+    lax.fori_loop(0, N, make_col_masks, 0)
+    choose_cols(cols_t, cols_s)
+    c2_src, c2_dst = (lambda p: cols_s.at[p]), (lambda p: cols_g.at[p])
+    start(COLS_X, "x", c2_src, c2_dst)
+    arrive(ROWS_Y, "y", r2_src, r2_dst)
+    arrive(COLS_X, "x", c2_src, c2_dst)
+    finish_halo(rows_s, rows_g, cols_s, cols_g, xpad)
 
     def filtered(src, flip, r):
         total = None
@@ -289,7 +334,7 @@
         square = pre * pre
         bend = jnp.tanh(0.7978845608 * pre * (1.0 + 0.044715 * square))
         half = 0.5 + 0.5 * bend
-        act_h[lanes(g), :] = (pre * half).astype(BF16)
+        act_h2[lanes(g), :] = (pre * half).astype(BF16)
         slope = half + (0.5 * 0.7978845608) * pre * (1.0 - bend * bend) * (
             1.0 + (3.0 * 0.044715) * square
         )
@@ -309,58 +354,70 @@
     d_src, d_dst = (lambda p: dconv_s.at[rows16(p), :]), (lambda p: dconv.at[:, lanes(p, 512)])
     start(DCONV, "z", d_src, d_dst)
     dconv[:, lanes(z, 512)] = dconv_s[rows16(z), :]
+
+    g_s[:, 0:64, :] = dot(dpre_h[...], feats[...], ((1,), (1,))).astype(BF16).reshape(N, 64, 128)
+    g_s[:, 64:128, :] = dot(act_h2[...], dz[...], ((1,), (1,))).astype(BF16).reshape(N, 64, 128)
+    gx_src, gx_dst = (lambda p: g_s.at[:, rows16(p), :]), (lambda p: g_x.at[p])
+    start(G_X, "x", gx_src, gx_dst)
+    g_x[q] = g_s[:, rows16(q), :]
+    branch_s[...] = dot(wo_all, act_h2[...], ((0,), (0,))).astype(BF16)
+    branch[:, lanes(z, 512)] = branch_s[rows16(z), :]
     folded = per_gain[:, 0:128] + per_gain[:, 128:256] + per_gain[:, 256:384] + per_gain[:, 384:512]
     gain_s[...] = folded.reshape(N, 16, 128)
-    n_src, n_dst = (lambda p: gain_s.at[p]), (lambda p: gains.at[p])
-    start(GAIN, "z", n_src, n_dst)
     gains[z] = gain_s[z]
 
-    g_s[:, 0:64, :] = dot(dpre_h[...], feats[...], ((1,), (1,))).astype(BF16).reshape(N, 64, 128)
-    g_s[:, 64:128, :] = dot(act_h[...], dz[...], ((1,), (1,))).astype(BF16).reshape(N, 64, 128)
-    gx_src, gx_dst = (lambda p: g_s.at[:, rows16(p), :]), (lambda p: g_x.at[p])
-    start(G_X, "x", gx_src, gx_dst)
-    branch_s[...] = dot(wo_all, act_h[...], ((0,), (0,))).astype(BF16)
-    b_src, b_dst = (lambda p: branch_s.at[rows16(p), :]), (lambda p: branch.at[:, lanes(p, 512)])
-    start(BRANCH, "z", b_src, b_dst)
-    branch[:, lanes(z, 512)] = branch_s[rows16(z), :]
-
     arrive(DCONV, "z", d_src, d_dst)
-    build_rim(dconv, drim)
-    e_src, e_dst = (lambda p: drim), (lambda p: dtable.at[p])
-    start(DRIM_Y, "y", e_src, e_dst)
-    dtable[y] = drim[...]
-    spread(dconv, dpad)
+    build_cols(dconv, d_cols)
+    e1_src, e1_dst = (lambda p: d_cols), (lambda p: d_cols_t.at[p])
+    start(D_COLS_Y, "y", e1_src, e1_dst)
+    build_rows(dconv, d_rows)
+    f1_src, f1_dst = (lambda p: d_rows), (lambda p: d_rows_t.at[p])
+    start(D_ROWS_X, "x", f1_src, f1_dst)
+    d_cols_t[y] = d_cols[...]
+    d_rows_t[q] = d_rows[...]
 
     arrive(G_X, "x", gx_src, gx_dst)
-    g_x[q] = g_s[:, rows16(q), :]
     g_xs[...] = jnp.sum(g_x[...].astype(F32), 0)
     gz_src, gz_dst = (lambda p: g_xs.at[p]), (lambda p: g_z.at[p])
     start(G_Z, "z", gz_src, gz_dst)
     g_z[z] = g_xs[z]
-
-    small = jnp.zeros((16, 128), F32)
-    for b in range(7):
-
-        def taps(r, carry, b=b):
-            moved = roll(dpad[pl.ds(3 + 8 * r, 8)], b - 3, 2)
-            return tuple(
-                carry[a] + jnp.sum(moved * xpad[pl.ds(8 * r + a, 8)], 0) for a in range(7)
-            )
-
-        column = lax.fori_loop(0, 8, taps, tuple(jnp.zeros((16, 128), F32) for _ in range(7)))
-        for a in range(7):
-            small = jnp.where(lane == a * 7 + b, jnp.sum(column[a], 1, keepdims=True), small)
+    n_src, n_dst = (lambda p: gain_s.at[p]), (lambda p: gains.at[p])
+    start(GAIN, "z", n_src, n_dst)
+    b_src, b_dst = (lambda p: branch_s.at[rows16(p), :]), (lambda p: branch.at[:, lanes(p, 512)])
+    start(BRANCH, "z", b_src, b_dst)
+    spread(dconv, dpad)
+
+    def filter_grad(small, columns):
+        for b in columns:
+
+            def taps(r, carry, b=b):
+                moved = roll(dpad[pl.ds(3 + 8 * r, 8)], b - 3, 2)
+                return tuple(
+                    carry[a] + jnp.sum(moved * xpad[pl.ds(8 * r + a, 8)], 0) for a in range(7)
+                )
+
+            column = lax.fori_loop(0, 8, taps, tuple(jnp.zeros((16, 128), F32) for _ in range(7)))
+            for a in range(7):
+                small = jnp.where(lane == a * 7 + b, jnp.sum(column[a], 1, keepdims=True), small)
+        return small
+
+    small = filter_grad(jnp.zeros((16, 128), F32), range(0, 4))
+    arrive(D_ROWS_X, "x", f1_src, f1_dst)
+    choose_rows(d_rows_t, d_rows_s)
+    f2_src, f2_dst = (lambda p: d_rows_s.at[p]), (lambda p: d_rows_g.at[p])
+    start(D_ROWS_Y, "y", f2_src, f2_dst)
+    small = filter_grad(small, range(4, 6))
+    arrive(D_COLS_Y, "y", e1_src, e1_dst)
+    choose_cols(d_cols_t, d_cols_s)
+    e2_src, e2_dst = (lambda p: d_cols_s.at[p]), (lambda p: d_cols_g.at[p])
+    start(D_COLS_X, "x", e2_src, e2_dst)
+    small = filter_grad(small, range(6, 7))
     arrive(GAIN, "z", n_src, n_dst)
     small = jnp.where(lane == 49, jnp.sum(jnp.sum(gains[...], 0), 1, keepdims=True), small)
     s_y[y] = small
     sy_src, sy_dst = (lambda p: s_y.at[y]), (lambda p: s_y.at[p])
     start(S_Y, "y", sy_src, sy_dst)
 
-    arrive(DRIM_Y, "y", e_src, e_dst)
-    choose(dtable, dhsend)
-    f_src, f_dst = (lambda p: dhsend.at[p]), (lambda p: dhbuf.at[p])
-    start(DRIM_X, "x", f_src, f_dst)
-
     arrive(G_Z, "z", gz_src, gz_dst)
     g_y[y] = jnp.sum(g_z[...], 0)
     gy_src, gy_dst = (lambda p: g_y.at[y]), (lambda p: g_y.at[p])
@@ -375,6 +432,11 @@
         return carry
 
     lax.fori_loop(0, 8, write_out, 0)
+    stores[0].start()
+
+    arrive(D_ROWS_Y, "y", f2_src, f2_dst)
+    arrive(D_COLS_X, "x", e2_src, e2_dst)
+    finish_halo(d_rows_s, d_rows_g, d_cols_s, d_cols_g, dpad)
 
     arrive(S_Y, "y", sy_src, sy_dst)
     s_x[q] = jnp.sum(s_y[...], 0)
@@ -385,9 +447,6 @@
     ga_src, ga_dst = (lambda p: g_all.at[q]), (lambda p: g_all.at[p])
     start(G_ALL, "x", ga_src, ga_dst)
 
-    arrive(DRIM_X, "x", f_src, f_dst)
-    finish_halo(dhsend, dhbuf, dpad)
-
     def backward(r, carry):
         tiles = filtered(dpad, True, r)
         for u in range(4):
@@ -396,32 +455,82 @@
         return carry
 
     lax.fori_loop(0, N, backward, 0)
+    stores[1].start()
 
     arrive(S_X, "x", sx_src, sx_dst)
-    small_out[...] = jnp.sum(s_x[...], 0)
+    small = jnp.sum(s_x[...], 0)
+    kgrad_out[...] = small[:, 0:49]
+    square16 = lax.broadcasted_iota(jnp.int32, (16, 16), 0) == lax.broadcasted_iota(
+        jnp.int32, (16, 16), 1
+    )
+    gain_out[...] = jnp.sum(
+        jnp.where(square16, jnp.broadcast_to(small[:, 49:50], (16, 16)), 0.0), 0, keepdims=True
+    )
+    stores[2].start()
+    stores[3].start()
     arrive(G_ALL, "x", ga_src, ga_dst)
-    wgrad_out[...] = g_all[...].reshape(128, 128)
+    both = g_all[...].reshape(128, 128)
+    w_in_out[...] = both[0:64]
+    w_out_out[...] = both[64:128]
+    stores[4].start()
+    stores[5].start()
     for stage, group, src, dst in sent:
         me = mine[group]
         peers(group, lambda p: copy(stage, group, src(p), dst(me), p, me).wait_send())
+    for store in stores:
+        store.wait()
+
+
+def finish_body(*refs):
+    count = len(refs) // 2
+    sems = refs[-1]
+    copies = [
+        pltpu.make_async_copy(refs[i], refs[count + i], sems.at[i]) for i in range(count)
+    ]
+    for move in copies:
+        move.start()
+    for move in copies:
+        move.wait()
 
 
 def body(activations, cotangent, kernel, gain, w_in, w_out, neighbours, land_mask):
-    vmem = pl.BlockSpec(memory_space=pltpu.VMEM)
-    smem = pl.BlockSpec(memory_space=pltpu.SMEM)
+    anywhere = pl.BlockSpec(memory_space=pl.ANY)
     scratch = [
+        ((16, 4096), BF16),
+        ((16, 4096), BF16),
+        ((16, 49), F32),
+        ((1, 128), F32),
+        ((64, 128), BF16),
+        ((64, 128), BF16),
+        ((1, 8), jnp.int32),
+        ((1, 4096), jnp.int32),
+        ((16, 4096), BF16),
+        ((16, 4096), BF16),
+        ((16, 49), F32),
+        ((1, 16), F32),
+        ((64, 128), F32),
+        ((64, 128), F32),
         ((70, 16, 128), F32),
         ((70, 16, 128), F32),
         ((49, 16, 128), F32),
-        ((128, 128), BF16),
-        ((128, 128), BF16),
-        ((N, 128, 128), BF16),
-        ((N, 128, 128), BF16),
+        ((64, 128), BF16),
+        ((80, 128), BF16),
+        ((48, 128), BF16),
+        ((64, 128), BF16),
+        ((N, 64, 128), BF16),
+        ((N, 80, 128), BF16),
+        ((N, 48, 128), BF16),
+        ((N, 64, 128), BF16),
         ((N, N, 8, 128), F32),
-        ((N, 128, 128), BF16),
-        ((N, 128, 128), BF16),
-        ((N, 128, 128), BF16),
-        ((N, 128, 128), BF16),
+        ((N, N, 8, 128), F32),
+        ((N, 48, 128), BF16),
+        ((N, 80, 128), BF16),
+        ((N, 48, 128), BF16),
+        ((N, 80, 128), BF16),
+        ((N, 48, 128), BF16),
+        ((N, 80, 128), BF16),
+        ((N, 48, 128), BF16),
+        ((N, 80, 128), BF16),
         ((N, 128, 128), BF16),
         ((16, 4096), BF16),
         ((16, 4096), BF16),
@@ -448,34 +557,44 @@
         ((N, 16, 128), F32),
         ((N, 16, 128), F32),
     ]
-    out, igrad, small, wgrad = pl.pallas_call(
+    shapes = [
+        jax.ShapeDtypeStruct((16, 4096), BF16),
+        jax.ShapeDtypeStruct((16, 4096), BF16),
+        jax.ShapeDtypeStruct((16, 49), F32),
+        jax.ShapeDtypeStruct((1, 16), F32),
+        jax.ShapeDtypeStruct((64, 128), F32),
+        jax.ShapeDtypeStruct((64, 128), F32),
+    ]
+    results = pl.pallas_call(
         kernel_body,
-        out_shape=(
-            jax.ShapeDtypeStruct((16, 4096), BF16),
-            jax.ShapeDtypeStruct((16, 4096), BF16),
-            jax.ShapeDtypeStruct((16, 128), F32),
-            jax.ShapeDtypeStruct((128, 128), F32),
-        ),
-        in_specs=[vmem, vmem, vmem, vmem, vmem, vmem, smem, vmem],
-        out_specs=[vmem] * 4,
+        out_shape=shapes,
+        in_specs=[anywhere] * 8,
+        out_specs=[anywhere] * 6,
         scratch_shapes=[pltpu.VMEM(shape, kind) for shape, kind in scratch]
-        + [pltpu.SemaphoreType.DMA((17, N)), pltpu.SemaphoreType.DMA((17, N))],
+        + [
+            pltpu.SemaphoreType.DMA((21, N)),
+            pltpu.SemaphoreType.DMA((21, N)),
+            pltpu.SemaphoreType.DMA((8,)),
+            pltpu.SemaphoreType.DMA((6,)),
+        ],
         compiler_params=pltpu.CompilerParams(
-            collective_id=0, has_side_effects=True, vmem_limit_bytes=40 * 1024 * 1024
+            collective_id=0, has_side_effects=True, vmem_limit_bytes=VMEM_LIMIT
         ),
         cost_estimate=pl.CostEstimate(flops=360000000, bytes_accessed=1000000, transcendentals=262144),
         name="block",
     )(
-        activations[0], cotangent[0], kernel, gain.reshape(1, 128), w_in, w_out, neighbours, land_mask,
+        activations[0], cotangent[0], kernel, gain.reshape(1, 128), w_in.T, w_out, neighbours, land_mask,
     )
-    return (
-        out[None],
-        igrad[None],
-        small[:, :49],
-        small[:, 49],
-        wgrad[:64].T,
-        wgrad[64:],
-    )
+    out, igrad, kgrad, ggrad, wigrad, wograd = pl.pallas_call(
+        finish_body,
+        out_shape=shapes,
+        in_specs=[anywhere] * 6,
+        out_specs=[anywhere] * 6,
+        scratch_shapes=[pltpu.SemaphoreType.DMA((6,))],
+        compiler_params=pltpu.CompilerParams(vmem_limit_bytes=VMEM_LIMIT),
+        name="results",
+    )(*results)
+    return (out[None], igrad[None], kgrad, ggrad.reshape(16), wigrad.T, wograd)
 
 
 def solution(mesh):

time: 74.6 us -> 77.2 us (1.035)
  Pallas kernels: 67.8 us -> 76.4 us
  local copies, waits for them, and re-layouts: 5.91 us -> 0 us
    pallas_call x1 -> x2, Pallas kernels: 67.8 us -> 76.4 us  [the longest x1 65.1 us: body(): pl.pallas_call(kernel_body, out_shape=shapes, in_specs=[anywhere] * 8, ou...]
    unnamed x18 -> x0, local copies, waits for them, and re-layouts: 4.58 us -> none
    slice x2 -> x0, local copies, waits for them, and re-layouts: 1.32 us -> none  [the longest x1 0.69 us: body(): small[:, 49]]
where the time goes in v2:
time: 77.2 us; the launch traced here: 77 us
  Pallas kernels  76.4 us (99%)
    pallas_call x1, Pallas kernels, body(): pl.pallas_call(kernel_body, out_shape=shapes, in_specs=[anywhere] * 8, ou...  65.1 us
    pallas_call x1, Pallas kernels, body(): pl.pallas_call(finish_body, out_shape=shapes, in_specs=[anywhere] * 6, ou...  11.3 us

profile of v2, /device:TPU:1, one launch (start us, length us, event | category | flops | bytes accessed | tf_op | source)
XLA Modules:
  0.0 77.0 jit_solution(13064720482517836812)
XLA Ops:
  0.6 65.1 %block.1 = (bf16[16,4096]{1,0:T(8,128)(2,1)}, bf16[16,4096]{1,0:T(8,128)(2,1)}, f32[16,49]{1,0:T(8,128)}, f32[1,16]{1,0:T(1,128)}, f32[64,128]{1,0:T(8,128)}, /*index=5*/f32[64,128]{1,0:T(8,128)}) custom-call(bf16[16,4096]{1,0:T(8,128)(2,1)} %bitcast.8, bf16[16,4096]{1,0:T(8,128)(2,1)} %bitcast.9, f32[16,49]{1,0:T(8,128)} %ker_h.1, f32[1,128]{1,0:T(1,128)} %bitcast.14, ...), custom_call_target="tpu_custom_call" | custom-call | flops 360000000 | bytes 1000000 | tf_op jit(solution)/shard_map/block/pallas_call | solution.py:568
  65.7 11.3 %results.1 = (bf16[16,4096]{1,0:T(8,128)(2,1)}, bf16[16,4096]{1,0:T(8,128)(2,1)}, f32[16,49]{1,0:T(8,128)}, f32[1,16]{1,0:T(1,128)}, f32[64,128]{1,0:T(8,128)}, /*index=5*/f32[64,128]{1,0:T(8,128)}) custom-call(bf16[16,4096]{1,0:T(8,128)(2,1)} %get-tuple-element.18.refs_0_, bf16[16,4096]{1,0:T(8,128)(2,1)} %get-tuple-element.19.refs_1_, ...), custom_call_target="tpu_custom_call" | custom-call | tf_op jit(solution)/shard_map/results/pallas_call | solution.py:588

commit v3 on v2

--- a/solution.py
+++ b/solution.py
@@ -37,6 +37,7 @@
     xpad, dpad, wb, rows, cols, d_rows, d_cols,
     rows_t, cols_t, d_rows_t, d_cols_t, row_masks, col_masks,
     rows_s, cols_s, d_rows_s, d_cols_s, rows_g, cols_g, d_rows_g, d_cols_g,
+    outers, sides, fixes, conv_c, back_c, sums,
     weights, masked, conv_r, means, convs, mean_all, dz, normed, feats, act_h2, dpre_h,
     dconv_s, dconv, branch_s, branch, gain_s, gains, g_s, g_x, g_xs, g_z, g_y, g_all, s_y, s_x,
     ssem, rsem, lsem, osem,
@@ -66,10 +67,10 @@
 
     def peers(group, step):
         def one(j, carry):
-            step(lax.rem(mine[group] + j, N))
+            step(lax.rem(mine[group] + 4 + (1 - 2 * lax.rem(j, 2)) * ((j + 1) // 2), N))
             return carry
 
-        lax.fori_loop(1, N, one, 0)
+        lax.fori_loop(0, N - 1, one, 0)
 
     sent = []
 
@@ -80,6 +81,12 @@
 
     def arrive(stage, group, src, dst):
         peers(group, lambda p: copy(stage, group, src(p), dst(p), p, p).wait_recv())
+
+    def settle():
+        for stage, group, src, dst in sent:
+            me = mine[group]
+            peers(group, lambda p: copy(stage, group, src(p), dst(me), p, me).wait_send())
+        sent.clear()
 
     lane = lax.broadcasted_iota(jnp.int32, (16, 128), 1)
     lane1 = lax.broadcasted_iota(jnp.int32, (1, 1, 128), 2)
@@ -129,14 +136,11 @@
         dst[32:48, :] = src[:, 3968:4096]
 
     def build_cols(src, dst):
-        def pack(block, carry):
+        for block in range(4):
             total = jnp.zeros((16, 128), F32)
             for t in range(8):
                 total = total + roll(jnp.where(edge, pair(src, block * 8 + t), 0.0), 8 * t, 1)
-            dst[rows16(block), :] = total.astype(BF16)
-            return carry
-
-        lax.fori_loop(0, 4, pack, 0)
+            dst[16 * block : 16 * block + 16, :] = total.astype(BF16)
 
     loads[0].wait()
     build_cols(act, cols)
@@ -179,15 +183,41 @@
         wb[tap] = jnp.broadcast_to(ker[:, tap : tap + 1], (16, 128))
 
     def spread(src, dst):
-        def rows(t, carry):
-            both = pair(src, t)
-            dst[3 + 2 * t] = jnp.where(low, both, 0.0)
-            dst[4 + 2 * t] = jnp.where(low, roll(both, 64, 1), 0.0)
+        def some(block, carry):
+            for u in range(8):
+                both = pair(src, 8 * block + u)
+                dst[3 + 16 * block + 2 * u] = jnp.where(low, both, 0.0)
+                dst[4 + 16 * block + 2 * u] = jnp.where(low, roll(both, 64, 1), 0.0)
             return carry
 
-        lax.fori_loop(0, 32, rows, 0)
+        for row in (0, 1, 2, 67, 68, 69):
+            dst[row] = jnp.zeros((16, 128), F32)
+        lax.fori_loop(0, 4, some, 0)
 
     spread(act, xpad)
+
+    def filtered(src, flip, r):
+        total = None
+        for b in range(7):
+            part = None
+            for a in range(7):
+                tap = (6 - a) * 7 + 6 - b if flip else a * 7 + b
+                term = wb[tap][None] * src[pl.ds(8 * r + a, 8)]
+                part = term if part is None else part + term
+            part = roll(part, 3 - b, 2)
+            total = part if total is None else total + part
+        return [jnp.where(low, total[2 * u], roll(total[2 * u + 1], 64, 1)) for u in range(4)]
+
+    def centre(src, flip, dst):
+        def some(r, carry):
+            tiles = filtered(src, flip, r)
+            for u in range(4):
+                dst[:, lanes(4 * r + u)] = tiles[u]
+            return carry
+
+        lax.fori_loop(0, N, some, 0)
+
+    centre(xpad, False, conv_c)
 
     index4 = lane1 // 4
     odd = (index4 & 1) == 1
@@ -241,26 +271,79 @@
             total = total + got[lax.rem(me + j, N), 16 * i : 16 * i + 16, :].astype(F32)
         return total
 
-    def finish_halo(own_rows, got_rows, own_cols, got_cols, dst):
+    block8, in8 = lane1 // 8, lane1 & 7
+    place = jnp.where(in8 < 4, (block8 + 8) & 15, (block8 + 1) & 15)
+    half, step = jnp.where(place < 8, 1, 0), place & 7
+
+    def gather_halo(own_rows, got_rows, own_cols, got_cols):
         top, mid, end = [added(y, own_rows, got_rows, i) for i in range(3)]
         corner = added(q, own_cols, got_cols, 4)
-
-        def outer(row, center, shift):
-            dst[row] = jnp.where(low, center, jnp.where(beside, roll(corner, shift, 1), 0.0))
-
-        outer(67, top, 64)
-        outer(68, roll(top, 64, 1), 0)
-        outer(69, mid, 56)
-        outer(0, roll(mid, 64, 1), 80)
-        outer(1, end, 8)
-        outer(2, roll(end, 64, 1), 72)
+        centres = (roll(mid, 64, 1), end, roll(end, 64, 1), top, roll(top, 64, 1), mid)
+        for i, shift in enumerate((80, 8, 72, 64, 0, 56)):
+            outers[i] = jnp.where(low, centres[i], jnp.where(beside, roll(corner, shift, 1), 0.0))
+        sides[0] = jnp.zeros((16, 128), F32)
+        sides[5] = jnp.zeros((16, 128), F32)
         for block in range(4):
-            side = added(q, own_cols, got_cols, block)
+            sides[1 + block] = added(q, own_cols, got_cols, block)
+
+    def fill_pad(dst):
+        for i, row in enumerate((0, 1, 2, 67, 68, 69)):
+            dst[row] = outers[i]
+        for block in range(4):
+            side = sides[1 + block]
             for t in range(8):
                 for o in range(2):
                     row = 3 + 16 * block + 2 * t + o
                     near = roll(side, 64 * (1 - o) - 8 * t, 1)
                     dst[row] = dst[row] + jnp.where(beside, near, 0.0)
+
+    def fix_rows(flip, dst):
+        def fixed(pieces):
+            total = None
+            for b in range(7):
+                part = None
+                for a, i in pieces:
+                    tap = (6 - a) * 7 + 6 - b if flip else a * 7 + b
+                    term = wb[tap] * outers[i]
+                    part = term if part is None else part + term
+                part = roll(part, 3 - b, 1)
+                total = part if total is None else total + part
+            return total
+
+        tops = [fixed([(a, i + a) for a in range(3 - i)]) for i in range(3)]
+        ends = [fixed([(6 - i + m, 3 + m) for m in range(i + 1)]) for i in range(3)]
+        zero = jnp.zeros((16, 128), F32)
+        for t, lower, upper in (
+            (0, tops[0], tops[1]), (1, tops[2], zero), (30, zero, ends[0]), (31, ends[1], ends[2]),
+        ):
+            at = slice(128 * t, 128 * t + 128)
+            dst[:, at] = dst[:, at] + jnp.where(low, lower, roll(upper, 64, 1))
+
+    def fix_cols(flip):
+        parts = [None] * 7
+        for a in range(7):
+            by = a - 3
+            moved = sides[1:5]
+            if by:
+                moved = jnp.zeros((4, 16, 128), F32)
+                for o in range(2):
+                    up = (o + by) // 2
+                    other = (o + by) - 2 * up
+                    for over in (-1, 0, 1):
+                        if over * up < 0 or (over and not up):
+                            continue
+                        fits = (half == o) & (step + up >= 8 * over) & (step + up < 8 * over + 8)
+                        from_ = roll(sides[1 + over : 5 + over], -8 * (up - 8 * over + 8 * (o - other)), 2)
+                        moved = jnp.where(fits, from_, moved)
+            for b in (0, 1, 2, 4, 5, 6):
+                tap = (6 - a) * 7 + 6 - b if flip else a * 7 + b
+                term = wb[tap][None] * moved
+                parts[b] = term if parts[b] is None else parts[b] + term
+        total = jnp.zeros((4, 16, 128), F32)
+        for b in (0, 1, 2, 4, 5, 6):
+            lands = in8 < 3 - b if b < 3 else in8 > 10 - b
+            total = total + jnp.where(lands, roll(parts[b], 3 - b, 2), 0.0)
+        fixes[...] = total
 
     arrive(ROWS_X, "x", r1_src, r1_dst)
     lax.fori_loop(0, N, make_row_masks, 0)
@@ -274,43 +357,29 @@
     start(COLS_X, "x", c2_src, c2_dst)
     arrive(ROWS_Y, "y", r2_src, r2_dst)
     arrive(COLS_X, "x", c2_src, c2_dst)
-    finish_halo(rows_s, rows_g, cols_s, cols_g, xpad)
-
-    def filtered(src, flip, r):
-        total = None
-        for b in range(7):
-            part = None
-            for a in range(7):
-                tap = (6 - a) * 7 + 6 - b if flip else a * 7 + b
-                term = wb[tap][None] * src[pl.ds(8 * r + a, 8)]
-                part = term if part is None else part + term
-            part = roll(part, 3 - b, 2)
-            total = part if total is None else total + part
-        return [jnp.where(low, total[2 * u], roll(total[2 * u + 1], 64, 1)) for u in range(4)]
+    gather_halo(rows_s, rows_g, cols_s, cols_g)
+    fix_rows(False, conv_c)
+    fix_cols(False)
 
     c_src, c_dst = (lambda p: conv_r.at[:, lanes(p, 512)]), (lambda p: convs.at[rows16(p), :])
     a_src, a_dst = (lambda p: means.at[:, lanes(p, 512)]), (lambda p: mean_all.at[p])
 
-    def forward(j, carry):
-        r = lax.rem(z + 1 + j, N)
-        tiles = filtered(xpad, False, r)
-        for u in range(4):
-            mean = jnp.sum(tiles[u], 0, keepdims=True) * (1.0 / 16)
-            conv_r[:, lanes(4 * r + u)] = (tiles[u] - mean).astype(BF16)
-            means[:, lanes(4 * r + u)] = mean
-
-        @pl.when(j < N - 1)
-        def _():
-            copy(CONV, "z", c_src(r), c_dst(z), r, z).start()
-            copy(MEANS, "z", a_src(r), a_dst(z), r, z).start()
-
+    def forward(block, carry):
+        for t in range(8):
+            at = lanes(8 * block + t)
+            whole = conv_c[:, at] + jnp.where(edge, roll(fixes[block], 64 - 8 * t, 1), 0.0)
+            mean = jnp.sum(whole, 0, keepdims=True) * (1.0 / 16)
+            conv_r[:, at] = (whole - mean).astype(BF16)
+            means[:, at] = mean
         return carry
 
-    lax.fori_loop(0, N, forward, 0)
-    sent.append((CONV, "z", c_src, c_dst))
-    sent.append((MEANS, "z", a_src, a_dst))
+    lax.fori_loop(0, 4, forward, 0)
+    start(CONV, "z", c_src, c_dst)
+    start(MEANS, "z", a_src, a_dst)
     convs[rows16(z), :] = conv_r[:, lanes(z, 512)]
     mean_all[z] = means[:, lanes(z, 512)]
+    fill_pad(xpad)
+    settle()
     arrive(CONV, "z", c_src, c_dst)
     arrive(MEANS, "z", a_src, a_dst)
 
@@ -345,6 +414,12 @@
     lax.fori_loop(0, 4, hidden, 0)
     wi_all = weights[:, 0:64, :].reshape(512, 128)
     wo_all = weights[:, 64:128, :].reshape(512, 128)
+    g_s[:, 0:64, :] = dot(dpre_h[...], feats[...], ((1,), (1,))).astype(BF16).reshape(N, 64, 128)
+    g_s[:, 64:128, :] = dot(act_h2[...], dz[...], ((1,), (1,))).astype(BF16).reshape(N, 64, 128)
+    gx_src, gx_dst = (lambda p: g_s.at[:, rows16(p), :]), (lambda p: g_x.at[p])
+    start(G_X, "x", gx_src, gx_dst)
+    g_x[q] = g_s[:, rows16(q), :]
+
     d_feat = dot(wi_all, dpre_h[...], ((0,), (0,)))
     per_gain = d_feat * normed[...]
     d_norm = d_feat * gain_col
@@ -354,18 +429,14 @@
     d_src, d_dst = (lambda p: dconv_s.at[rows16(p), :]), (lambda p: dconv.at[:, lanes(p, 512)])
     start(DCONV, "z", d_src, d_dst)
     dconv[:, lanes(z, 512)] = dconv_s[rows16(z), :]
-
-    g_s[:, 0:64, :] = dot(dpre_h[...], feats[...], ((1,), (1,))).astype(BF16).reshape(N, 64, 128)
-    g_s[:, 64:128, :] = dot(act_h2[...], dz[...], ((1,), (1,))).astype(BF16).reshape(N, 64, 128)
-    gx_src, gx_dst = (lambda p: g_s.at[:, rows16(p), :]), (lambda p: g_x.at[p])
-    start(G_X, "x", gx_src, gx_dst)
-    g_x[q] = g_s[:, rows16(q), :]
+    gain_sum = jnp.sum(per_gain, 1, keepdims=True)
+    gain_s[...] = jnp.sum(jnp.where(diagonal, gain_sum, 0.0), 0, keepdims=True)
+    n_src, n_dst = (lambda p: gain_s), (lambda p: gains.at[p])
+    start(GAIN, "z", n_src, n_dst)
+    gains[z] = gain_s[...]
+
     branch_s[...] = dot(wo_all, act_h2[...], ((0,), (0,))).astype(BF16)
     branch[:, lanes(z, 512)] = branch_s[rows16(z), :]
-    folded = per_gain[:, 0:128] + per_gain[:, 128:256] + per_gain[:, 256:384] + per_gain[:, 384:512]
-    gain_s[...] = folded.reshape(N, 16, 128)
-    gains[z] = gain_s[z]
-
     arrive(DCONV, "z", d_src, d_dst)
     build_cols(dconv, d_cols)
     e1_src, e1_dst = (lambda p: d_cols), (lambda p: d_cols_t.at[p])
@@ -377,66 +448,47 @@
     d_rows_t[q] = d_rows[...]
 
     arrive(G_X, "x", gx_src, gx_dst)
-    g_xs[...] = jnp.sum(g_x[...].astype(F32), 0)
+    g_xs[...] = jnp.sum(g_x[...].astype(F32), 0).astype(BF16)
     gz_src, gz_dst = (lambda p: g_xs.at[p]), (lambda p: g_z.at[p])
     start(G_Z, "z", gz_src, gz_dst)
     g_z[z] = g_xs[z]
-    n_src, n_dst = (lambda p: gain_s.at[p]), (lambda p: gains.at[p])
-    start(GAIN, "z", n_src, n_dst)
-    b_src, b_dst = (lambda p: branch_s.at[rows16(p), :]), (lambda p: branch.at[:, lanes(p, 512)])
-    start(BRANCH, "z", b_src, b_dst)
     spread(dconv, dpad)
 
-    def filter_grad(small, columns):
-        for b in columns:
-
-            def taps(r, carry, b=b):
-                moved = roll(dpad[pl.ds(3 + 8 * r, 8)], b - 3, 2)
-                return tuple(
-                    carry[a] + jnp.sum(moved * xpad[pl.ds(8 * r + a, 8)], 0) for a in range(7)
-                )
-
-            column = lax.fori_loop(0, 8, taps, tuple(jnp.zeros((16, 128), F32) for _ in range(7)))
+    def taps(r, carry):
+        for b in range(7):
+            moved = roll(dpad[pl.ds(3 + 8 * r, 8)], b - 3, 2)
             for a in range(7):
-                small = jnp.where(lane == a * 7 + b, jnp.sum(column[a], 1, keepdims=True), small)
-        return small
-
-    small = filter_grad(jnp.zeros((16, 128), F32), range(0, 4))
+                sums[a * 7 + b] += jnp.sum(moved * xpad[pl.ds(8 * r + a, 8)], 0)
+        return carry
+
+    sums[...] = jnp.zeros((49, 16, 128), F32)
+    lax.fori_loop(0, 8, taps, 0)
+    small = jnp.zeros((16, 128), F32)
+    for tap in range(49):
+        small = jnp.where(lane == tap, jnp.sum(sums[tap], 1, keepdims=True), small)
+    arrive(GAIN, "z", n_src, n_dst)
+    sub = lax.broadcasted_iota(jnp.int32, (16, 128), 0)
+    gain_mine = jnp.where(lane == sub + 16 * z, jnp.broadcast_to(jnp.sum(gains[...], 0), (16, 128)), 0.0)
+    small = jnp.where(lane == 49, jnp.sum(gain_mine, 1, keepdims=True), small)
+    s_y[y] = small
+    sy_src, sy_dst = (lambda p: s_y.at[y]), (lambda p: s_y.at[p])
+    start(S_Y, "y", sy_src, sy_dst)
+
     arrive(D_ROWS_X, "x", f1_src, f1_dst)
     choose_rows(d_rows_t, d_rows_s)
     f2_src, f2_dst = (lambda p: d_rows_s.at[p]), (lambda p: d_rows_g.at[p])
     start(D_ROWS_Y, "y", f2_src, f2_dst)
-    small = filter_grad(small, range(4, 6))
+    arrive(G_Z, "z", gz_src, gz_dst)
+    g_y[y] = jnp.sum(g_z[...].astype(F32), 0)
+    gy_src, gy_dst = (lambda p: g_y.at[y]), (lambda p: g_y.at[p])
+    start(G_Y, "y", gy_src, gy_dst)
     arrive(D_COLS_Y, "y", e1_src, e1_dst)
     choose_cols(d_cols_t, d_cols_s)
     e2_src, e2_dst = (lambda p: d_cols_s.at[p]), (lambda p: d_cols_g.at[p])
     start(D_COLS_X, "x", e2_src, e2_dst)
-    small = filter_grad(small, range(6, 7))
-    arrive(GAIN, "z", n_src, n_dst)
-    small = jnp.where(lane == 49, jnp.sum(jnp.sum(gains[...], 0), 1, keepdims=True), small)
-    s_y[y] = small
-    sy_src, sy_dst = (lambda p: s_y.at[y]), (lambda p: s_y.at[p])
-    start(S_Y, "y", sy_src, sy_dst)
-
-    arrive(G_Z, "z", gz_src, gz_dst)
-    g_y[y] = jnp.sum(g_z[...], 0)
-    gy_src, gy_dst = (lambda p: g_y.at[y]), (lambda p: g_y.at[p])
-    start(G_Y, "y", gy_src, gy_dst)
-
-    arrive(BRANCH, "z", b_src, b_dst)
-
-    def write_out(t, carry):
-        at = lanes(t, 512)
-        kept = mask[:, at].astype(F32)
-        out[:, at] = (act[:, at].astype(F32) + kept * branch[:, at].astype(F32)).astype(BF16)
-        return carry
-
-    lax.fori_loop(0, 8, write_out, 0)
-    stores[0].start()
-
-    arrive(D_ROWS_Y, "y", f2_src, f2_dst)
-    arrive(D_COLS_X, "x", e2_src, e2_dst)
-    finish_halo(d_rows_s, d_rows_g, d_cols_s, d_cols_g, dpad)
+    b_src, b_dst = (lambda p: branch_s.at[rows16(p), :]), (lambda p: branch.at[:, lanes(p, 512)])
+    start(BRANCH, "z", b_src, b_dst)
+    centre(dpad, True, back_c)
 
     arrive(S_Y, "y", sy_src, sy_dst)
     s_x[q] = jnp.sum(s_y[...], 0)
@@ -447,16 +499,34 @@
     ga_src, ga_dst = (lambda p: g_all.at[q]), (lambda p: g_all.at[p])
     start(G_ALL, "x", ga_src, ga_dst)
 
-    def backward(r, carry):
-        tiles = filtered(dpad, True, r)
-        for u in range(4):
-            at = lanes(4 * r + u)
-            igrad[:, at] = (cot[:, at].astype(F32) + tiles[u]).astype(BF16)
+    arrive(D_ROWS_Y, "y", f2_src, f2_dst)
+    arrive(D_COLS_X, "x", e2_src, e2_dst)
+    gather_halo(d_rows_s, d_rows_g, d_cols_s, d_cols_g)
+    fix_rows(True, back_c)
+    fix_cols(True)
+
+    def backward(block, carry):
+        for t in range(8):
+            at = lanes(8 * block + t)
+            whole = back_c[:, at] + jnp.where(edge, roll(fixes[block], 64 - 8 * t, 1), 0.0)
+            igrad[:, at] = (cot[:, at].astype(F32) + whole).astype(BF16)
         return carry
 
-    lax.fori_loop(0, N, backward, 0)
+    lax.fori_loop(0, 4, backward, 0)
     stores[1].start()
 
+    arrive(BRANCH, "z", b_src, b_dst)
+
+    def write_out(t, carry):
+        at = lanes(t, 512)
+        kept = mask[:, at].astype(F32)
+        out[:, at] = (act[:, at].astype(F32) + kept * branch[:, at].astype(F32)).astype(BF16)
+        return carry
+
+    lax.fori_loop(0, 8, write_out, 0)
+    stores[0].start()
+
+    settle()
     arrive(S_X, "x", sx_src, sx_dst)
     small = jnp.sum(s_x[...], 0)
     kgrad_out[...] = small[:, 0:49]
@@ -474,23 +544,24 @@
     w_out_out[...] = both[64:128]
     stores[4].start()
     stores[5].start()
-    for stage, group, src, dst in sent:
-        me = mine[group]
-        peers(group, lambda p: copy(stage, group, src(p), dst(me), p, me).wait_send())
+    settle()
     for store in stores:
         store.wait()
 
 
 def finish_body(*refs):
-    count = len(refs) // 2
-    sems = refs[-1]
-    copies = [
-        pltpu.make_async_copy(refs[i], refs[count + i], sems.at[i]) for i in range(count)
-    ]
-    for move in copies:
-        move.start()
-    for move in copies:
-        move.wait()
+    count = (len(refs) - 2) // 3
+    arrays, results, held = refs[:count], refs[count : 2 * count], refs[2 * count : 3 * count]
+    came, went = refs[-2:]
+    loads = [pltpu.make_async_copy(arrays[i], held[i], came.at[i]) for i in range(count)]
+    stores = [pltpu.make_async_copy(held[i], results[i], went.at[i]) for i in range(count)]
+    for load in loads:
+        load.start()
+    for load, store in zip(loads, stores):
+        load.wait()
+        store.start()
+    for store in stores:
+        store.wait()
 
 
 def body(activations, cotangent, kernel, gain, w_in, w_out, neighbours, land_mask):
@@ -531,6 +602,12 @@
         ((N, 80, 128), BF16),
         ((N, 48, 128), BF16),
         ((N, 80, 128), BF16),
+        ((6, 16, 128), F32),
+        ((6, 16, 128), F32),
+        ((4, 16, 128), F32),
+        ((16, 4096), F32),
+        ((16, 4096), F32),
+        ((49, 16, 128), F32),
         ((N, 128, 128), BF16),
         ((16, 4096), BF16),
         ((16, 4096), BF16),
@@ -546,12 +623,12 @@
         ((16, 4096), BF16),
         ((128, 512), BF16),
         ((16, 4096), BF16),
-        ((N, 16, 128), F32),
-        ((N, 16, 128), F32),
+        ((1, 128), F32),
+        ((N, 1, 128), F32),
         ((N, 128, 128), BF16),
         ((N, N, 16, 128), BF16),
-        ((N, 16, 128), F32),
-        ((N, 16, 128), F32),
+        ((N, 16, 128), BF16),
+        ((N, 16, 128), BF16),
         ((N, 16, 128), F32),
         ((N, 16, 128), F32),
         ((N, 16, 128), F32),
@@ -590,7 +667,8 @@
         out_shape=shapes,
         in_specs=[anywhere] * 6,
         out_specs=[anywhere] * 6,
-        scratch_shapes=[pltpu.SemaphoreType.DMA((6,))],
+        scratch_shapes=[pltpu.VMEM(result.shape, result.dtype) for result in shapes]
+        + [pltpu.SemaphoreType.DMA((6,)), pltpu.SemaphoreType.DMA((6,))],
         compiler_params=pltpu.CompilerParams(vmem_limit_bytes=VMEM_LIMIT),
         name="results",
     )(*results)

time: 77.2 us -> 62.7 us (0.81)
  Pallas kernels: 76.4 us -> 61.9 us
    pallas_call x1, Pallas kernels: 11.3 us -> 1.75 us  [body(): pl.pallas_call(finish_body, out_shape=shapes, in_specs=[anywhere] * 6, ou...]
    pallas_call x1, Pallas kernels: 65.1 us -> 60.2 us  [body(): pl.pallas_call(kernel_body, out_shape=shapes, in_specs=[anywhere] * 8, ou...]
where the time goes in v3:
time: 62.7 us; the launch traced here: 62.6 us
  Pallas kernels  61.9 us (99%)
  between operations  0.64 us (1%)
    pallas_call x1, Pallas kernels, body(): pl.pallas_call(kernel_body, out_shape=shapes, in_specs=[anywhere] * 8, ou...  60.2 us
    pallas_call x1, Pallas kernels, body(): pl.pallas_call(finish_body, out_shape=shapes, in_specs=[anywhere] * 6, ou...  1.75 us

profile of v3, /device:TPU:1, one launch (start us, length us, event | category | flops | bytes accessed | tf_op | source)
XLA Modules:
  0.0 62.6 jit_solution(8670209489655176888)
XLA Ops:
  0.6 60.2 %block.1 = (bf16[16,4096]{1,0:T(8,128)(2,1)}, bf16[16,4096]{1,0:T(8,128)(2,1)}, f32[16,49]{1,0:T(8,128)}, f32[1,16]{1,0:T(1,128)}, f32[64,128]{1,0:T(8,128)}, /*index=5*/f32[64,128]{1,0:T(8,128)}) custom-call(bf16[16,4096]{1,0:T(8,128)(2,1)} %bitcast.8, bf16[16,4096]{1,0:T(8,128)(2,1)} %bitcast.9, f32[16,49]{1,0:T(8,128)} %ker_h.1, f32[1,128]{1,0:T(1,128)} %bitcast.14, ...), custom_call_target="tpu_custom_call" | custom-call | flops 360000000 | bytes 1000000 | tf_op jit(solution)/shard_map/block/pallas_call | solution.py:645
  60.8 1.8 %results.1 = (bf16[16,4096]{1,0:T(8,128)(2,1)}, bf16[16,4096]{1,0:T(8,128)(2,1)}, f32[16,49]{1,0:T(8,128)}, f32[1,16]{1,0:T(1,128)}, f32[64,128]{1,0:T(8,128)}, /*index=5*/f32[64,128]{1,0:T(8,128)}) custom-call(bf16[16,4096]{1,0:T(8,128)(2,1)} %get-tuple-element.18.refs_0_, bf16[16,4096]{1,0:T(8,128)(2,1)} %get-tuple-element.19.refs_1_, ...), custom_call_target="tpu_custom_call" | custom-call | tf_op jit(solution)/shard_map/results/pallas_call | solution.py:665

commit v4 on v3

--- a/solution.py
+++ b/solution.py
@@ -13,8 +13,8 @@
 
 (
     ROWS_X, COLS_Y, ROWS_Y, COLS_X, D_ROWS_X, D_COLS_Y, D_ROWS_Y, D_COLS_X,
-    WEIGHTS, MASKED, CONV, MEANS, DCONV, BRANCH, GAIN, G_X, G_Z, G_Y, G_ALL, S_Y, S_X,
-) = range(21)
+    WEIGHTS, MASKED, CONV, MEANS, DCONV, BRANCH, GAIN, G_X, G_X2, G_Z, G_Y, G_ALL, S_Y, S_X,
+) = range(22)
 
 
 def dot(a, b, dims):
@@ -113,8 +113,6 @@
         (w_in_h, w_in), (w_out_h, w_out), (ker_h, ker), (gain_h, gain),
     ]
     loads = [pltpu.make_async_copy(src, dst, lsem.at[i]) for i, (src, dst) in enumerate(inputs)]
-    for load in loads:
-        load.start()
     results = [
         (out, out_h), (igrad, igrad_h), (kgrad_out, kgrad_h), (gain_out, ggrad_h),
         (w_in_out, w_in_grad_h), (w_out_out, w_out_grad_h),
@@ -129,6 +127,8 @@
                 barrier, inc=1, device_id=device(group, p), device_id_type=pl.DeviceIdType.MESH
             ),
         )
+    for load in loads:
+        load.start()
 
     def build_rows(src, dst):
         dst[0:16, :] = src[:, 0:128]
@@ -152,7 +152,9 @@
     )
     listed = jnp.broadcast_to(listed, (16, 128)).astype(BF16)
     rows[48:64, :] = listed
-    cols[64:80, :] = listed
+    for k in range(8):
+        spare = jnp.broadcast_to(nbr[0:1, k : k + 1].astype(F32), (16, 128)).astype(BF16)
+        cols[0:16, :] = jnp.where(lane == 8 * k + 3, spare, cols[0:16, :])
 
     pl.semaphore_wait(barrier, 3 * (N - 1))
     c1_src, c1_dst = (lambda p: cols), (lambda p: cols_t.at[p])
@@ -208,14 +210,14 @@
             total = part if total is None else total + part
         return [jnp.where(low, total[2 * u], roll(total[2 * u + 1], 64, 1)) for u in range(4)]
 
-    def centre(src, flip, dst):
+    def centre(src, flip, dst, first=0, last=N):
         def some(r, carry):
             tiles = filtered(src, flip, r)
             for u in range(4):
                 dst[:, lanes(4 * r + u)] = tiles[u]
             return carry
 
-        lax.fori_loop(0, N, some, 0)
+        lax.fori_loop(first, last, some, 0)
 
     centre(xpad, False, conv_c)
 
@@ -224,12 +226,10 @@
     in_top = window_in(index4, (0, 15, 16, 31, 2, 17))
     in_bottom = window_in(index4, (28, 11, 14, 29, 30, 13))
 
-    def listed_as(table, first, number):
-        near = (table[:, first : first + 16, :].astype(F32) == number.astype(F32)).astype(F32)
-        return [near[:, k : k + 1, :] for k in range(8)]
-
     def make_col_masks(d, carry):
-        m = listed_as(cols_t, 64, y * N + d)
+        number = (y * N + d).astype(F32)
+        near = (cols_t[:, 0:16, :].astype(F32)[:, 0:1, :] == number).astype(F32)
+        m = [jnp.broadcast_to(near[:, :, 8 * k + 3 : 8 * k + 4], (N, 1, 128)) for k in range(8)]
         col_masks[d, :, 0:1, :] = jnp.where(odd, m[4], m[3])
         col_masks[d, :, 1:2, :] = jnp.where(
             in_top, jnp.where(odd, m[2], m[0]), jnp.where(in_bottom, jnp.where(odd, m[7], m[5]), 0.0)
@@ -237,7 +237,9 @@
         return carry
 
     def make_row_masks(d, carry):
-        m = listed_as(rows_t, 48, d * N + q)
+        number = (d * N + q).astype(F32)
+        near = (rows_t[:, 48:64, :].astype(F32) == number).astype(F32)
+        m = [near[:, k : k + 1, :] for k in range(8)]
         row_masks[d, :, 0:1, :] = m[1]
         row_masks[d, :, 1:2, :] = jnp.where(lane1 < 64, m[1], m[6])
         row_masks[d, :, 2:3, :] = m[6]
@@ -320,30 +322,32 @@
             dst[:, at] = dst[:, at] + jnp.where(low, lower, roll(upper, 64, 1))
 
     def fix_cols(flip):
-        parts = [None] * 7
-        for a in range(7):
-            by = a - 3
-            moved = sides[1:5]
-            if by:
-                moved = jnp.zeros((4, 16, 128), F32)
-                for o in range(2):
-                    up = (o + by) // 2
-                    other = (o + by) - 2 * up
-                    for over in (-1, 0, 1):
-                        if over * up < 0 or (over and not up):
-                            continue
-                        fits = (half == o) & (step + up >= 8 * over) & (step + up < 8 * over + 8)
-                        from_ = roll(sides[1 + over : 5 + over], -8 * (up - 8 * over + 8 * (o - other)), 2)
-                        moved = jnp.where(fits, from_, moved)
+        for first in (0, 2):
+            parts = [None] * 7
+            for a in range(7):
+                by = a - 3
+                moved = sides[first + 1 : first + 3]
+                if by:
+                    moved = jnp.zeros((2, 16, 128), F32)
+                    for o in range(2):
+                        up = (o + by) // 2
+                        other = (o + by) - 2 * up
+                        for over in (-1, 0, 1):
+                            if over * up < 0 or (over and not up):
+                                continue
+                            fits = (half == o) & (step + up >= 8 * over) & (step + up < 8 * over + 8)
+                            source = sides[first + 1 + over : first + 3 + over]
+                            shift = -8 * (up - 8 * over + 8 * (o - other))
+                            moved = jnp.where(fits, roll(source, shift, 2), moved)
+                for b in (0, 1, 2, 4, 5, 6):
+                    tap = (6 - a) * 7 + 6 - b if flip else a * 7 + b
+                    term = wb[tap][None] * moved
+                    parts[b] = term if parts[b] is None else parts[b] + term
+            total = jnp.zeros((2, 16, 128), F32)
             for b in (0, 1, 2, 4, 5, 6):
-                tap = (6 - a) * 7 + 6 - b if flip else a * 7 + b
-                term = wb[tap][None] * moved
-                parts[b] = term if parts[b] is None else parts[b] + term
-        total = jnp.zeros((4, 16, 128), F32)
-        for b in (0, 1, 2, 4, 5, 6):
-            lands = in8 < 3 - b if b < 3 else in8 > 10 - b
-            total = total + jnp.where(lands, roll(parts[b], 3 - b, 2), 0.0)
-        fixes[...] = total
+                lands = in8 < 3 - b if b < 3 else in8 > 10 - b
+                total = total + jnp.where(lands, roll(parts[b], 3 - b, 2), 0.0)
+            fixes[first : first + 2] = total
 
     arrive(ROWS_X, "x", r1_src, r1_dst)
     lax.fori_loop(0, N, make_row_masks, 0)
@@ -411,15 +415,19 @@
         dpre_h[lanes(g), :] = (d_act * slope).astype(BF16)
         return carry
 
-    lax.fori_loop(0, 4, hidden, 0)
+    def weight_grads(part, stage):
+        units, groups = slice(256 * part, 256 * part + 256), pl.ds(4 * part, 4)
+        g_s[groups, 0:64, :] = dot(dpre_h[units, :], feats[...], ((1,), (1,))).astype(BF16).reshape(4, 64, 128)
+        g_s[groups, 64:128, :] = dot(act_h2[units, :], dz[...], ((1,), (1,))).astype(BF16).reshape(4, 64, 128)
+        src, dst = (lambda p: g_s.at[groups, rows16(p), :]), (lambda p: g_x.at[p, groups])
+        start(stage, "x", src, dst)
+        return src, dst
+
+    lax.fori_loop(0, 2, hidden, 0)
+    gx_src, gx_dst = weight_grads(0, G_X)
+    lax.fori_loop(2, 4, hidden, 0)
     wi_all = weights[:, 0:64, :].reshape(512, 128)
     wo_all = weights[:, 64:128, :].reshape(512, 128)
-    g_s[:, 0:64, :] = dot(dpre_h[...], feats[...], ((1,), (1,))).astype(BF16).reshape(N, 64, 128)
-    g_s[:, 64:128, :] = dot(act_h2[...], dz[...], ((1,), (1,))).astype(BF16).reshape(N, 64, 128)
-    gx_src, gx_dst = (lambda p: g_s.at[:, rows16(p), :]), (lambda p: g_x.at[p])
-    start(G_X, "x", gx_src, gx_dst)
-    g_x[q] = g_s[:, rows16(q), :]
-
     d_feat = dot(wi_all, dpre_h[...], ((0,), (0,)))
     per_gain = d_feat * normed[...]
     d_norm = d_feat * gain_col
@@ -429,6 +437,8 @@
     d_src, d_dst = (lambda p: dconv_s.at[rows16(p), :]), (lambda p: dconv.at[:, lanes(p, 512)])
     start(DCONV, "z", d_src, d_dst)
     dconv[:, lanes(z, 512)] = dconv_s[rows16(z), :]
+    gx2_src, gx2_dst = weight_grads(1, G_X2)
+    g_x[q] = g_s[:, rows16(q), :]
     gain_sum = jnp.sum(per_gain, 1, keepdims=True)
     gain_s[...] = jnp.sum(jnp.where(diagonal, gain_sum, 0.0), 0, keepdims=True)
     n_src, n_dst = (lambda p: gain_s), (lambda p: gains.at[p])
@@ -437,6 +447,12 @@
 
     branch_s[...] = dot(wo_all, act_h2[...], ((0,), (0,))).astype(BF16)
     branch[:, lanes(z, 512)] = branch_s[rows16(z), :]
+    arrive(G_X, "x", gx_src, gx_dst)
+    arrive(G_X2, "x", gx2_src, gx2_dst)
+    g_xs[...] = jnp.sum(g_x[...].astype(F32), 0).astype(BF16)
+    gz_src, gz_dst = (lambda p: g_xs.at[p]), (lambda p: g_z.at[p])
+    start(G_Z, "z", gz_src, gz_dst)
+    g_z[z] = g_xs[z]
     arrive(DCONV, "z", d_src, d_dst)
     build_cols(dconv, d_cols)
     e1_src, e1_dst = (lambda p: d_cols), (lambda p: d_cols_t.at[p])
@@ -447,11 +463,6 @@
     d_cols_t[y] = d_cols[...]
     d_rows_t[q] = d_rows[...]
 
-    arrive(G_X, "x", gx_src, gx_dst)
-    g_xs[...] = jnp.sum(g_x[...].astype(F32), 0).astype(BF16)
-    gz_src, gz_dst = (lambda p: g_xs.at[p]), (lambda p: g_z.at[p])
-    start(G_Z, "z", gz_src, gz_dst)
-    g_z[z] = g_xs[z]
     spread(dconv, dpad)
 
     def taps(r, carry):
@@ -474,26 +485,26 @@
     sy_src, sy_dst = (lambda p: s_y.at[y]), (lambda p: s_y.at[p])
     start(S_Y, "y", sy_src, sy_dst)
 
+    arrive(G_Z, "z", gz_src, gz_dst)
+    g_y[y] = jnp.sum(g_z[...].astype(F32), 0)
+    gy_src, gy_dst = (lambda p: g_y.at[y]), (lambda p: g_y.at[p])
+    start(G_Y, "y", gy_src, gy_dst)
     arrive(D_ROWS_X, "x", f1_src, f1_dst)
     choose_rows(d_rows_t, d_rows_s)
     f2_src, f2_dst = (lambda p: d_rows_s.at[p]), (lambda p: d_rows_g.at[p])
     start(D_ROWS_Y, "y", f2_src, f2_dst)
-    arrive(G_Z, "z", gz_src, gz_dst)
-    g_y[y] = jnp.sum(g_z[...].astype(F32), 0)
-    gy_src, gy_dst = (lambda p: g_y.at[y]), (lambda p: g_y.at[p])
-    start(G_Y, "y", gy_src, gy_dst)
     arrive(D_COLS_Y, "y", e1_src, e1_dst)
     choose_cols(d_cols_t, d_cols_s)
     e2_src, e2_dst = (lambda p: d_cols_s.at[p]), (lambda p: d_cols_g.at[p])
     start(D_COLS_X, "x", e2_src, e2_dst)
     b_src, b_dst = (lambda p: branch_s.at[rows16(p), :]), (lambda p: branch.at[:, lanes(p, 512)])
     start(BRANCH, "z", b_src, b_dst)
-    centre(dpad, True, back_c)
-
+    centre(dpad, True, back_c, 0, 4)
     arrive(S_Y, "y", sy_src, sy_dst)
     s_x[q] = jnp.sum(s_y[...], 0)
     sx_src, sx_dst = (lambda p: s_x.at[q]), (lambda p: s_x.at[p])
     start(S_X, "x", sx_src, sx_dst)
+    centre(dpad, True, back_c, 4, N)
     arrive(G_Y, "y", gy_src, gy_dst)
     g_all[q] = jnp.sum(g_y[...], 0)
     ga_src, ga_dst = (lambda p: g_all.at[q]), (lambda p: g_all.at[p])
@@ -585,11 +596,11 @@
         ((70, 16, 128), F32),
         ((49, 16, 128), F32),
         ((64, 128), BF16),
-        ((80, 128), BF16),
+        ((64, 128), BF16),
         ((48, 128), BF16),
         ((64, 128), BF16),
         ((N, 64, 128), BF16),
-        ((N, 80, 128), BF16),
+        ((N, 64, 128), BF16),
         ((N, 48, 128), BF16),
         ((N, 64, 128), BF16),
         ((N, N, 8, 128), F32),
@@ -649,8 +660,8 @@
         out_specs=[anywhere] * 6,
         scratch_shapes=[pltpu.VMEM(shape, kind) for shape, kind in scratch]
         + [
-            pltpu.SemaphoreType.DMA((21, N)),
-            pltpu.SemaphoreType.DMA((21, N)),
+            pltpu.SemaphoreType.DMA((22, N)),
+            pltpu.SemaphoreType.DMA((22, N)),
             pltpu.SemaphoreType.DMA((8,)),
             pltpu.SemaphoreType.DMA((6,)),
         ],

time: 62.7 us -> 61.4 us (0.979)
  Pallas kernels: 61.9 us -> 60.6 us
    pallas_call x1, Pallas kernels: 60.2 us -> 58.8 us  [body(): pl.pallas_call(kernel_body, out_shape=shapes, in_specs=[anywhere] * 8, ou...]
where the time goes in v4:
time: 61.4 us; the launch traced here: 61.2 us
  Pallas kernels  60.6 us (99%)
  between operations  0.64 us (1%)
    pallas_call x1, Pallas kernels, body(): pl.pallas_call(kernel_body, out_shape=shapes, in_specs=[anywhere] * 8, ou...  58.8 us
    pallas_call x1, Pallas kernels, body(): pl.pallas_call(finish_body, out_shape=shapes, in_specs=[anywhere] * 6, ou...  1.75 us

profile of v4, /device:TPU:1, one launch (start us, length us, event | category | flops | bytes accessed | tf_op | source)
XLA Modules:
  0.0 61.2 jit_solution(3705096145470104664)
XLA Ops:
  0.6 58.8 %block.1 = (bf16[16,4096]{1,0:T(8,128)(2,1)}, bf16[16,4096]{1,0:T(8,128)(2,1)}, f32[16,49]{1,0:T(8,128)}, f32[1,16]{1,0:T(1,128)}, f32[64,128]{1,0:T(8,128)}, /*index=5*/f32[64,128]{1,0:T(8,128)}) custom-call(bf16[16,4096]{1,0:T(8,128)(2,1)} %bitcast.8, bf16[16,4096]{1,0:T(8,128)(2,1)} %bitcast.9, f32[16,49]{1,0:T(8,128)} %ker_h.1, f32[1,128]{1,0:T(1,128)} %bitcast.14, ...), custom_call_target="tpu_custom_call" | custom-call | flops 360000000 | bytes 1000000 | tf_op jit(solution)/shard_map/block/pallas_call | solution.py:656
  59.5 1.8 %results.1 = (bf16[16,4096]{1,0:T(8,128)(2,1)}, bf16[16,4096]{1,0:T(8,128)(2,1)}, f32[16,49]{1,0:T(8,128)}, f32[1,16]{1,0:T(1,128)}, f32[64,128]{1,0:T(8,128)}, /*index=5*/f32[64,128]{1,0:T(8,128)}) custom-call(bf16[16,4096]{1,0:T(8,128)(2,1)} %get-tuple-element.18.refs_0_, bf16[16,4096]{1,0:T(8,128)(2,1)} %get-tuple-element.19.refs_1_, ...), custom_call_target="tpu_custom_call" | custom-call | tf_op jit(solution)/shard_map/results/pallas_call | solution.py:676

commit v5 on v4

--- a/solution.py
+++ b/solution.py
@@ -14,7 +14,8 @@
 (
     ROWS_X, COLS_Y, ROWS_Y, COLS_X, D_ROWS_X, D_COLS_Y, D_ROWS_Y, D_COLS_X,
     WEIGHTS, MASKED, CONV, MEANS, DCONV, BRANCH, GAIN, G_X, G_X2, G_Z, G_Y, G_ALL, S_Y, S_X,
-) = range(22)
+    FIX_COLS, FIX_ROWS, SIBLING,
+) = range(25)
 
 
 def dot(a, b, dims):
@@ -37,7 +38,7 @@
     xpad, dpad, wb, rows, cols, d_rows, d_cols,
     rows_t, cols_t, d_rows_t, d_cols_t, row_masks, col_masks,
     rows_s, cols_s, d_rows_s, d_cols_s, rows_g, cols_g, d_rows_g, d_cols_g,
-    outers, sides, fixes, conv_c, back_c, sums,
+    outers, sides, fixes, row_fix, fix_g, row_fix_g, added_in, back_c, sums,
     weights, masked, conv_r, means, convs, mean_all, dz, normed, feats, act_h2, dpre_h,
     dconv_s, dconv, branch_s, branch, gain_s, gains, g_s, g_x, g_xs, g_z, g_y, g_all, s_y, s_x,
     ssem, rsem, lsem, osem,
@@ -66,11 +67,8 @@
         )
 
     def peers(group, step):
-        def one(j, carry):
-            step(lax.rem(mine[group] + 4 + (1 - 2 * lax.rem(j, 2)) * ((j + 1) // 2), N))
-            return carry
-
-        lax.fori_loop(0, N - 1, one, 0)
+        for offset in (4, 3, 5, 2, 6, 1, 7):
+            step((mine[group] + offset) & (N - 1))
 
     sent = []
 
@@ -166,10 +164,15 @@
 
     for load in loads[2:]:
         load.wait()
-    weights[z, 0:64, :] = w_in[...]
-    weights[z, 64:128, :] = w_out[...]
-    w_src, w_dst = (lambda p: weights.at[z]), (lambda p: weights.at[p])
+    core = q & 1
+    mine_half = pl.ds(pl.multiple_of(64 * core, 64), 64)
+    weights[z, mine_half, :] = jnp.where(core == 0, w_in[...], w_out[...])
+    w_src, w_dst = (lambda p: weights.at[z, mine_half]), (lambda p: weights.at[p, mine_half])
     start(WEIGHTS, "z", w_src, w_dst)
+
+    def sibling(half, slot):
+        part = weights.at[:, half]
+        return copy(SIBLING, "x", part, part, q ^ 1, slot)
 
     def mask_cot(t, carry):
         kept = mask[:, lanes(t, 512)].astype(F32)
@@ -219,7 +222,21 @@
 
         lax.fori_loop(first, last, some, 0)
 
-    centre(xpad, False, conv_c)
+    def forward(r, carry):
+        tiles = filtered(xpad, False, r)
+        for u in range(4):
+            mean = jnp.sum(tiles[u], 0, keepdims=True) * (1.0 / 16)
+            conv_r[:, lanes(4 * r + u)] = (tiles[u] - mean).astype(BF16)
+            means[:, lanes(4 * r + u)] = mean
+        return carry
+
+    lax.fori_loop(0, N, forward, 0)
+    c_src, c_dst = (lambda p: conv_r.at[:, lanes(p, 512)]), (lambda p: convs.at[rows16(p), :])
+    a_src, a_dst = (lambda p: means.at[:, lanes(p, 512)]), (lambda p: mean_all.at[p])
+    start(CONV, "z", c_src, c_dst)
+    start(MEANS, "z", a_src, a_dst)
+    convs[rows16(z), :] = conv_r[:, lanes(z, 512)]
+    mean_all[z] = means[:, lanes(z, 512)]
 
     index4 = lane1 // 4
     odd = (index4 & 1) == 1
@@ -299,7 +316,7 @@
                     near = roll(side, 64 * (1 - o) - 8 * t, 1)
                     dst[row] = dst[row] + jnp.where(beside, near, 0.0)
 
-    def fix_rows(flip, dst):
+    def fix_rows(flip):
         def fixed(pieces):
             total = None
             for b in range(7):
@@ -315,11 +332,10 @@
         tops = [fixed([(a, i + a) for a in range(3 - i)]) for i in range(3)]
         ends = [fixed([(6 - i + m, 3 + m) for m in range(i + 1)]) for i in range(3)]
         zero = jnp.zeros((16, 128), F32)
-        for t, lower, upper in (
-            (0, tops[0], tops[1]), (1, tops[2], zero), (30, zero, ends[0]), (31, ends[1], ends[2]),
-        ):
-            at = slice(128 * t, 128 * t + 128)
-            dst[:, at] = dst[:, at] + jnp.where(low, lower, roll(upper, 64, 1))
+        return [
+            jnp.where(low, lower, roll(upper, 64, 1))
+            for lower, upper in ((tops[0], tops[1]), (tops[2], zero), (zero, ends[0]), (ends[1], ends[2]))
+        ]
 
     def fix_cols(flip):
         for first in (0, 2):
@@ -359,37 +375,58 @@
     choose_cols(cols_t, cols_s)
     c2_src, c2_dst = (lambda p: cols_s.at[p]), (lambda p: cols_g.at[p])
     start(COLS_X, "x", c2_src, c2_dst)
+    arrive(WEIGHTS, "z", w_src, w_dst)
+    sibling(mine_half, q).start()
     arrive(ROWS_Y, "y", r2_src, r2_dst)
     arrive(COLS_X, "x", c2_src, c2_dst)
     gather_halo(rows_s, rows_g, cols_s, cols_g)
-    fix_rows(False, conv_c)
     fix_cols(False)
-
-    c_src, c_dst = (lambda p: conv_r.at[:, lanes(p, 512)]), (lambda p: convs.at[rows16(p), :])
-    a_src, a_dst = (lambda p: means.at[:, lanes(p, 512)]), (lambda p: mean_all.at[p])
-
-    def forward(block, carry):
-        for t in range(8):
-            at = lanes(8 * block + t)
-            whole = conv_c[:, at] + jnp.where(edge, roll(fixes[block], 64 - 8 * t, 1), 0.0)
-            mean = jnp.sum(whole, 0, keepdims=True) * (1.0 / 16)
-            conv_r[:, at] = (whole - mean).astype(BF16)
-            means[:, at] = mean
-        return carry
-
-    lax.fori_loop(0, 4, forward, 0)
-    start(CONV, "z", c_src, c_dst)
-    start(MEANS, "z", a_src, a_dst)
-    convs[rows16(z), :] = conv_r[:, lanes(z, 512)]
-    mean_all[z] = means[:, lanes(z, 512)]
+    k_src, k_dst = (lambda p: fixes.at[p // 2]), (lambda p: fix_g.at[rows16(p), :])
+    start(FIX_COLS, "z", k_src, k_dst)
+    for i, tile_fix in enumerate(fix_rows(False)):
+        row_fix[i // 2, :, 128 * (i % 2) : 128 * (i % 2) + 128] = tile_fix
+
+    def row_copy(end, slot):
+        return copy(FIX_ROWS, "z", row_fix.at[end], row_fix_g.at[slot], (N - 1) * end, slot)
+
+    for end in range(2):
+
+        @pl.when(z != (N - 1) * end)
+        def _():
+            row_copy(end, z).start()
+
     fill_pad(xpad)
     settle()
+    for end in range(2):
+
+        @pl.when(z != (N - 1) * end)
+        def _():
+            row_copy(end, z).wait_send()
+
+    sibling(mine_half, q).wait_send()
+    sibling(pl.ds(pl.multiple_of(64 - 64 * core, 64), 64), q ^ 1).wait_recv()
+    fix_g[rows16(z), :] = fixes[z // 2]
     arrive(CONV, "z", c_src, c_dst)
     arrive(MEANS, "z", a_src, a_dst)
+    arrive(FIX_COLS, "z", k_src, k_dst)
+    turned = pltpu.roll(fix_g[...], lax.rem(128 - 32 * (z & 1), 128), 1)
+    border = edge[0:1, :]
+    for u in range(4):
+        added_in[:, 128 * u : 128 * u + 128] = jnp.where(border, roll(turned, 64 - 8 * u, 1), 0.0)
+    for end in range(2):
+
+        @pl.when(z == (N - 1) * end)
+        def _():
+            row_fix_g[z] = row_fix[end]
+            peers("z", lambda p: row_copy(end, p).wait_recv())
+            at = slice(256 * end, 256 * end + 256)
+            added_in[:, at] = added_in[:, at] + row_fix_g[...].reshape(128, 256)
 
     local = mean_all[...]
-    mean = jnp.sum(local, 0) * (1.0 / N)
-    centred = (convs[...].astype(F32).reshape(N, 16, 512) + (local - mean[None])).reshape(128, 512)
+    extra = added_in[...]
+    mean = jnp.sum(local, 0) * (1.0 / N) + jnp.sum(extra, 0, keepdims=True) * (1.0 / 128)
+    centred = (convs[...].astype(F32) + extra).reshape(N, 16, 512) + (local - mean[None])
+    centred = centred.reshape(128, 512)
     rstd = lax.rsqrt(jnp.sum(centred * centred, 0, keepdims=True) * (1.0 / 128) + EPS)
     normed[...] = centred * rstd
     diagonal = lax.broadcasted_iota(jnp.int32, (128, 128), 0) == lax.broadcasted_iota(
@@ -397,7 +434,6 @@
     )
     gain_col = jnp.sum(jnp.where(diagonal, jnp.broadcast_to(gain[...], (128, 128)), 0.0), 1, keepdims=True)
     feats[...] = (normed[...] * gain_col).astype(BF16)
-    arrive(WEIGHTS, "z", w_src, w_dst)
     arrive(MASKED, "z", m_src, m_dst)
 
     def hidden(g, carry):
@@ -513,7 +549,9 @@
     arrive(D_ROWS_Y, "y", f2_src, f2_dst)
     arrive(D_COLS_X, "x", e2_src, e2_dst)
     gather_halo(d_rows_s, d_rows_g, d_cols_s, d_cols_g)
-    fix_rows(True, back_c)
+    for t, tile_fix in zip((0, 1, 30, 31), fix_rows(True)):
+        at = slice(128 * t, 128 * t + 128)
+        back_c[:, at] = back_c[:, at] + tile_fix
     fix_cols(True)
 
     def backward(block, carry):
@@ -616,7 +654,10 @@
         ((6, 16, 128), F32),
         ((6, 16, 128), F32),
         ((4, 16, 128), F32),
-        ((16, 4096), F32),
+        ((2, 16, 256), F32),
+        ((128, 128), F32),
+        ((N, 16, 256), F32),
+        ((128, 512), F32),
         ((16, 4096), F32),
         ((49, 16, 128), F32),
         ((N, 128, 128), BF16),
@@ -660,8 +701,8 @@
         out_specs=[anywhere] * 6,
         scratch_shapes=[pltpu.VMEM(shape, kind) for shape, kind in scratch]
         + [
-            pltpu.SemaphoreType.DMA((22, N)),
-            pltpu.SemaphoreType.DMA((22, N)),
+            pltpu.SemaphoreType.DMA((25, N)),
+            pltpu.SemaphoreType.DMA((25, N)),
             pltpu.SemaphoreType.DMA((8,)),
             pltpu.SemaphoreType.DMA((6,)),
         ],

time: 61.4 us -> 58.7 us (0.956)
  Pallas kernels: 60.6 us -> 57.9 us
    pallas_call x1, Pallas kernels: 58.8 us -> 56.2 us  [body(): pl.pallas_call(kernel_body, out_shape=shapes, in_specs=[anywhere] * 8, ou...]
where the time goes in v5:
time: 58.7 us; the launch traced here: 58.6 us
  Pallas kernels  57.9 us (99%)
  between operations  0.64 us (1%)
    pallas_call x1, Pallas kernels, body(): pl.pallas_call(kernel_body, out_shape=shapes, in_specs=[anywhere] * 8, ou...  56.2 us
    pallas_call x1, Pallas kernels, body(): pl.pallas_call(finish_body, out_shape=shapes, in_specs=[anywhere] * 6, ou...  1.75 us

profile of v5, /device:TPU:1, one launch (start us, length us, event | category | flops | bytes accessed | tf_op | source)
XLA Modules:
  0.0 58.6 jit_solution(7200363449893936553)
XLA Ops:
  0.6 56.2 %block.1 = (bf16[16,4096]{1,0:T(8,128)(2,1)}, bf16[16,4096]{1,0:T(8,128)(2,1)}, f32[16,49]{1,0:T(8,128)}, f32[1,16]{1,0:T(1,128)}, f32[64,128]{1,0:T(8,128)}, /*index=5*/f32[64,128]{1,0:T(8,128)}) custom-call(bf16[16,4096]{1,0:T(8,128)(2,1)} %bitcast.8, bf16[16,4096]{1,0:T(8,128)(2,1)} %bitcast.9, f32[16,49]{1,0:T(8,128)} %ker_h.1, f32[1,128]{1,0:T(1,128)} %bitcast.14, ...), custom_call_target="tpu_custom_call" | custom-call | flops 360000000 | bytes 1000000 | tf_op jit(solution)/shard_map/block/pallas_call | solution.py:697
  56.8 1.8 %results.1 = (bf16[16,4096]{1,0:T(8,128)(2,1)}, bf16[16,4096]{1,0:T(8,128)(2,1)}, f32[16,49]{1,0:T(8,128)}, f32[1,16]{1,0:T(1,128)}, f32[64,128]{1,0:T(8,128)}, /*index=5*/f32[64,128]{1,0:T(8,128)}) custom-call(bf16[16,4096]{1,0:T(8,128)(2,1)} %get-tuple-element.18.refs_0_, bf16[16,4096]{1,0:T(8,128)(2,1)} %get-tuple-element.19.refs_1_, ...), custom_call_target="tpu_custom_call" | custom-call | tf_op jit(solution)/shard_map/results/pallas_call | solution.py:717

commit v6 on v5

--- a/solution.py
+++ b/solution.py
@@ -213,14 +213,14 @@
             total = part if total is None else total + part
         return [jnp.where(low, total[2 * u], roll(total[2 * u + 1], 64, 1)) for u in range(4)]
 
-    def centre(src, flip, dst, first=0, last=N):
+    def centre(src, flip, dst):
         def some(r, carry):
             tiles = filtered(src, flip, r)
             for u in range(4):
                 dst[:, lanes(4 * r + u)] = tiles[u]
             return carry
 
-        lax.fori_loop(first, last, some, 0)
+        lax.fori_loop(0, N, some, 0)
 
     def forward(r, carry):
         tiles = filtered(xpad, False, r)
@@ -270,7 +270,7 @@
                 dst[d, 16 * part : 16 * part + 16, :] = total.astype(BF16)
             return carry
 
-        lax.fori_loop(0, N, one, 0)
+        lax.fori_loop(0, N, one, 0, unroll=2)
 
     def choose_cols(src, dst):
         def one(d, carry):
@@ -282,7 +282,7 @@
             dst[d, 64:80, :] = jnp.sum(col_masks[d, :, 1:2, :] * block, 0).astype(BF16)
             return carry
 
-        lax.fori_loop(0, N, one, 0)
+        lax.fori_loop(0, N, one, 0, unroll=2)
 
     def added(me, own, got, i):
         total = own[me, 16 * i : 16 * i + 16, :].astype(F32)
@@ -366,12 +366,12 @@
             fixes[first : first + 2] = total
 
     arrive(ROWS_X, "x", r1_src, r1_dst)
-    lax.fori_loop(0, N, make_row_masks, 0)
+    lax.fori_loop(0, N, make_row_masks, 0, unroll=2)
     choose_rows(rows_t, rows_s)
     r2_src, r2_dst = (lambda p: rows_s.at[p]), (lambda p: rows_g.at[p])
     start(ROWS_Y, "y", r2_src, r2_dst)
     arrive(COLS_Y, "y", c1_src, c1_dst)
-    lax.fori_loop(0, N, make_col_masks, 0)
+    lax.fori_loop(0, N, make_col_masks, 0, unroll=2)
     choose_cols(cols_t, cols_s)
     c2_src, c2_dst = (lambda p: cols_s.at[p]), (lambda p: cols_g.at[p])
     start(COLS_X, "x", c2_src, c2_dst)
@@ -535,12 +535,11 @@
     start(D_COLS_X, "x", e2_src, e2_dst)
     b_src, b_dst = (lambda p: branch_s.at[rows16(p), :]), (lambda p: branch.at[:, lanes(p, 512)])
     start(BRANCH, "z", b_src, b_dst)
-    centre(dpad, True, back_c, 0, 4)
+    centre(dpad, True, back_c)
     arrive(S_Y, "y", sy_src, sy_dst)
     s_x[q] = jnp.sum(s_y[...], 0)
     sx_src, sx_dst = (lambda p: s_x.at[q]), (lambda p: s_x.at[p])
     start(S_X, "x", sx_src, sx_dst)
-    centre(dpad, True, back_c, 4, N)
     arrive(G_Y, "y", gy_src, gy_dst)
     g_all[q] = jnp.sum(g_y[...], 0)
     ga_src, ga_dst = (lambda p: g_all.at[q]), (lambda p: g_all.at[p])

time: 58.7 us -> 58.3 us (level)
  no operation moved by 1% of the time
where the time goes in v6:
time: 58.3 us; the launch traced here: 58.2 us
  Pallas kernels  57.5 us (99%)
  between operations  0.64 us (1%)
    pallas_call x1, Pallas kernels, body(): pl.pallas_call(kernel_body, out_shape=shapes, in_specs=[anywhere] * 8, ou...  55.8 us
    pallas_call x1, Pallas kernels, body(): pl.pallas_call(finish_body, out_shape=shapes, in_specs=[anywhere] * 6, ou...  1.75 us

profile of v6, /device:TPU:1, one launch (start us, length us, event | category | flops | bytes accessed | tf_op | source)
XLA Modules:
  0.0 58.2 jit_solution(4941659297627320442)
XLA Ops:
  0.6 55.8 %block.1 = (bf16[16,4096]{1,0:T(8,128)(2,1)}, bf16[16,4096]{1,0:T(8,128)(2,1)}, f32[16,49]{1,0:T(8,128)}, f32[1,16]{1,0:T(1,128)}, f32[64,128]{1,0:T(8,128)}, /*index=5*/f32[64,128]{1,0:T(8,128)}) custom-call(bf16[16,4096]{1,0:T(8,128)(2,1)} %bitcast.8, bf16[16,4096]{1,0:T(8,128)(2,1)} %bitcast.9, f32[16,49]{1,0:T(8,128)} %ker_h.1, f32[1,128]{1,0:T(1,128)} %bitcast.14, ...), custom_call_target="tpu_custom_call" | custom-call | flops 360000000 | bytes 1000000 | tf_op jit(solution)/shard_map/block/pallas_call | solution.py:696
  56.4 1.8 %results.1 = (bf16[16,4096]{1,0:T(8,128)(2,1)}, bf16[16,4096]{1,0:T(8,128)(2,1)}, f32[16,49]{1,0:T(8,128)}, f32[1,16]{1,0:T(1,128)}, f32[64,128]{1,0:T(8,128)}, /*index=5*/f32[64,128]{1,0:T(8,128)}) custom-call(bf16[16,4096]{1,0:T(8,128)(2,1)} %get-tuple-element.18.refs_0_, bf16[16,4096]{1,0:T(8,128)(2,1)} %get-tuple-element.19.refs_1_, ...), custom_call_target="tpu_custom_call" | custom-call | tf_op jit(solution)/shard_map/results/pallas_call | solution.py:716
